TPU v7x, 128 devices: a whole 4x4x4 slice. The times are simulated.
128 devices in a mesh: gx: 8 (over z, core), gy: 16 (over x, y).
Axes of the slice: x: 4, y: 4, z: 4, core: 2. Of those that a mesh axis runs over, the one named last changes fastest.
Arguments:
- velocity: float32 [256, 512, 3, 256], P('gx', 'gy'), may hold values from -6 to 6
- fiber_loads: float32 [3, 786432], P(None, ('gx', 'gy')), may hold values from -96 to 96
- fractions: float32 [3, 786432], P(None, ('gx', 'gy')), may hold values from 0 to 1
- corners: int32 [3, 786432], P(None, ('gx', 'gy')), may hold values from 0 to 511, as said below
- neighbours: int32 [786432], P(('gx', 'gy')), may hold values from 0 to 6143
- counts: int32 [16384], P(('gx', 'gy')), may hold values from 1 to 48, as said below
Outputs:
- velocity_next: float32 [256, 512, 3, 256], P('gx', 'gy')
- fiber_velocity: float32 [3, 786432], P(None, ('gx', 'gy'))
Inputs may be any that keep to these rules, and one draw needn't show every extreme that they name: `counts`: in every draw some destination device receives 48 live slots from every source device. For a slot whose destination device has x block a and y block b: corners[0] is a * 32 + o mod 256 with o from -2 to 30, corners[1] is b * 32 + o mod 512 with o from -2 to 30, corners[2] any cell along z.
All inputs are finite; a program needn't handle non-finite values.
Results may differ from a plain program's by a relative error of at most 0.0029.
Values may be sent and summed in bfloat16 or wider, within the bound.
A program may use at most 128 MiB of HBM per device.

v0:
```python
import functools

import jax
import jax.numpy as jnp
from jax import lax
from jax.experimental import pallas as pl
from jax.experimental.pallas import tpu as pltpu
from jax.sharding import PartitionSpec as P

viscosity = 0.15
GX, GY = 8, 16
DEVICES = GX * GY
CAP = 48
SLOTS = CAP * DEVICES
CELLS = 32
NZ = 256
EXT = 40
ROWS = 36 * EXT
BLOCKS = CAP // 2
MESH = pl.DeviceIdType.MESH
VMEM = pl.BlockSpec(memory_space=pltpu.VMEM)
ANY = pl.BlockSpec(memory_space=pl.ANY)
f32, bf16, i32 = jnp.float32, jnp.bfloat16, jnp.int32


def params(mib=16, **more):
    return pltpu.CompilerParams(vmem_limit_bytes=mib * 2**20, **more)


def prep_kernel(loads_ref, frac_ref, corner_ref, partner_ref, counts_ref, out_ref, flat_ref, pos_ref):
    def flat_rows(ref, c):
        for r in range(CAP):
            flat_ref[r : r + 1, :] = ref[c : c + 1, 128 * r : 128 * r + 128].astype(f32)
        return flat_ref[...]

    lane = lax.broadcasted_iota(i32, (CAP, 128), 1)
    flat_id = lax.broadcasted_iota(i32, (CAP, 128), 0) * 128 + lane
    bucket = (flat_id * 43691) >> 21
    partner = partner_ref[...]
    high, low = partner >> 7, partner & 127
    whole = (CELLS * GX, CELLS * GY, NZ)
    for c in range(3):
        fraction = flat_rows(frac_ref, c)
        corner = flat_rows(corner_ref, c)
        loads = flat_rows(loads_ref, c)
        position = corner + fraction
        flat_ref[...] = position
        gathered = jnp.zeros((CAP, 128), f32)
        for r in range(CAP):
            row = jnp.broadcast_to(flat_ref[r : r + 1, :], (CAP, 128))
            taken = jnp.take_along_axis(row, low, axis=1, mode="promise_in_bounds")
            gathered = jnp.where(high == r, taken, gathered)
        forcing = loads + (2.0 / whole[c]) * (gathered - position)
        pos_ref[c * CAP : c * CAP + CAP, :] = forcing
        cell = corner.astype(i32)
        if c == 0:
            cell = (cell - (bucket >> 4) * CELLS + 4) & (whole[0] - 1)
        if c == 1:
            cell = (cell - (bucket & 15) * CELLS + 4) & (whole[1] - 1)
        pos_ref[(3 + c) * CAP : (3 + c) * CAP + CAP, :] = cell.astype(f32) + fraction

    lane = lax.broadcasted_iota(i32, (16, 128), 1)
    for j in range(8):
        row0, lane0 = divmod(CAP * j, 128)
        live = (lane & 63) < counts_ref[pl.ds(j, 16, stride=8), :]

        def piece(v, target):
            part = pos_ref[pl.ds(v * CAP + row0, 16, stride=3), :]
            if lane0 + CAP > 128:
                later = pos_ref[pl.ds(v * CAP + row0 + 1, 16, stride=3), :]
                part = jnp.where(lane >= lane0, part, later)
            shift = (target - lane0) % 128
            return pltpu.roll(part, shift, 1) if shift else part

        for pair in range(3):
            row = jnp.where(lane < 64, piece(2 * pair, 0), piece(2 * pair + 1, 64))
            if pair == 0:
                row = jnp.where(live, row, 0.0)
            if pair == 1:
                row = jnp.where(live | (lane >= 64), row, 0.0)
            out_ref[pl.ds(4 * j + pair, 16, stride=32), :] = row
        out_ref[pl.ds(4 * j + 3, 16, stride=32), :] = jnp.zeros((16, 128), f32)


def greet(peers):
    barrier = pltpu.get_barrier_semaphore()
    for peer in peers:
        pl.semaphore_signal(barrier, inc=1, device_id=peer, device_id_type=MESH)
    pl.semaphore_wait(barrier, len(peers))


def two_stage(first_axis, first, second_axis, second, x_ref, out_ref, mid_ref, send1, recv1, send2, recv2, here):
    me1, me2 = lax.axis_index(first_axis), lax.axis_index(second_axis)
    greet(
        [{first_axis: lax.rem(me1 + k, first)} for k in range(1, first)]
        + [{second_axis: lax.rem(me2 + k, second)} for k in range(1, second)]
    )
    copies = []
    for k in range(1, first):
        peer = lax.rem(me1 + k, first)
        copy = pltpu.make_async_remote_copy(
            src_ref=x_ref.at[peer],
            dst_ref=mid_ref.at[me1],
            send_sem=send1.at[k],
            recv_sem=recv1.at[k],
            device_id={first_axis: peer},
            device_id_type=MESH,
        )
        copy.start()
        copies.append(copy)
    own = pltpu.make_async_copy(x_ref.at[me1], mid_ref.at[me1], here.at[0])
    own.start()
    own.wait()
    for copy in copies:
        copy.wait_recv()
    for k in range(1, second):
        peer = lax.rem(me2 + k, second)
        copy = pltpu.make_async_remote_copy(
            src_ref=mid_ref.at[:, peer],
            dst_ref=out_ref.at[me2],
            send_sem=send2.at[k],
            recv_sem=recv2.at[k],
            device_id={second_axis: peer},
            device_id_type=MESH,
        )
        copy.start()
        copies.append(copy)
    own = pltpu.make_async_copy(mid_ref.at[:, me2], out_ref.at[me2], here.at[1])
    own.start()
    own.wait()
    for copy in copies[first - 1 :]:
        copy.wait_recv()
    for copy in copies:
        copy.wait_send()


def exchange(x, first_axis, first, second_axis, second, rows, identity):
    kernel = functools.partial(two_stage, first_axis, first, second_axis, second)
    return pl.pallas_call(
        kernel,
        out_shape=jax.ShapeDtypeStruct((second, first, rows, 128), f32),
        in_specs=[VMEM],
        out_specs=VMEM,
        scratch_shapes=[
            pltpu.VMEM((first, second, rows, 128), f32),
            pltpu.SemaphoreType.DMA((first,)),
            pltpu.SemaphoreType.DMA((first,)),
            pltpu.SemaphoreType.DMA((second,)),
            pltpu.SemaphoreType.DMA((second,)),
            pltpu.SemaphoreType.DMA((2,)),
        ],
        compiler_params=params(collective_id=identity, has_side_effects=True),
    )(x.reshape(first, second, rows, 128))


SIDES = ((-1, 0), (1, 0), (0, -1), (0, 1), (-1, -1), (-1, 1), (1, -1), (1, 1))
LOW, HIGH = (2, 8), (32, 38)


def side_rows(side):
    dx, dy = side
    return 6 * EXT if dy == 0 else 36 * 8 if dx == 0 else 6 * 8


def halo_kernel(*refs):
    sent, got, (send, recv) = refs[:8], refs[8:16], refs[16:]
    x, y = lax.axis_index("gx"), lax.axis_index("gy")
    peers = [(lax.rem(x + dx + GX, GX), lax.rem(y + dy + GY, GY)) for dx, dy in SIDES]
    greet(peers)
    copies = []
    for k in range(8):
        copy = pltpu.make_async_remote_copy(
            src_ref=sent[k],
            dst_ref=got[k],
            send_sem=send.at[k],
            recv_sem=recv.at[k],
            device_id=peers[k],
            device_id_type=MESH,
        )
        copy.start()
        copies.append(copy)
    for copy in copies:
        copy.wait_recv()
    for copy in copies:
        copy.wait_send()


def halo_exchange(strips):
    return pl.pallas_call(
        halo_kernel,
        out_shape=[jax.ShapeDtypeStruct(s.shape, s.dtype) for s in strips],
        in_specs=[VMEM] * 8,
        out_specs=[VMEM] * 8,
        scratch_shapes=[pltpu.SemaphoreType.DMA((8,)), pltpu.SemaphoreType.DMA((8,))],
        compiler_params=params(collective_id=1, has_side_effects=True),
    )(*strips)


def point_row(ref, base, block):
    return jnp.concatenate([ref[pl.ds(base + 2 * block, 1), :], ref[pl.ds(base + 2 * block + 1, 1), :]], axis=1)


def table(wts_ref, cell_ref, dim, block, length):
    corner = point_row(cell_ref, dim * CAP, block)
    delta = lax.broadcasted_iota(i32, (length, 256), 0) - corner
    if dim == 2:
        delta = delta & (NZ - 1)
    result = jnp.zeros((length, 256), f32)
    for k in range(4):
        result = jnp.where(delta == k, point_row(wts_ref, (4 * dim + k) * CAP, block), result)
    return result


def plane_rows(wts_ref, cell_ref, block, store):
    along_x = table(wts_ref, cell_ref, 0, block, EXT)
    along_y = table(wts_ref, cell_ref, 1, block, EXT)
    for i in range(18):
        x = 2 + 2 * i
        both = jnp.concatenate([along_y * along_x[x : x + 1], along_y * along_x[x + 1 : x + 2]], axis=0)
        store(80 * i, both.astype(bf16))


def spread_kernel(recv_ref, velocity_ref, field_ref, wts_ref, cell_ref, *refs):
    strips, (values_ref, plane_ref, push_ref) = refs[:8], refs[8:]
    for pair in range(3):
        values_ref[128 * pair : 128 * pair + 128, :] = recv_ref[pl.ds(pair, 128, stride=4), :].T
    for dim in range(3):
        position = values_ref[64 * (3 + dim) : 64 * (3 + dim) + CAP, :]
        corner = jnp.floor(position)
        angle = (0.5 * jnp.pi) * (position - corner)
        sine, cosine = jnp.sin(angle), jnp.cos(angle)
        cell_ref[dim * CAP : dim * CAP + CAP, :] = corner.astype(i32)
        for k, term in enumerate((-sine, cosine, sine, -cosine)):
            at = (4 * dim + k) * CAP
            wts_ref[at : at + CAP, :] = 0.25 * (1.0 + term)

    def fill(block, _):
        columns = pl.ds(pl.multiple_of(block * 256, 256), 256)

        def store(row, both):
            plane_ref[row : row + 80, columns] = both

        plane_rows(wts_ref, cell_ref, block, store)
        depth = table(wts_ref, cell_ref, 2, block, NZ)
        for c in range(3):
            push_ref[c, :, columns] = (depth * point_row(values_ref, 64 * c, block)).astype(bf16)
        return 0

    lax.fori_loop(0, BLOCKS, fill, 0)

    def component(c, _):
        base = c * EXT
        empty = jnp.zeros((2, EXT, NZ), f32)
        field_ref[pl.ds(base, 2)] = empty
        field_ref[pl.ds(base + 38, 2)] = empty
        push = push_ref[c]

        for half in range(2):
            part = lax.dot_general(
                plane_ref[720 * half : 720 * half + 720, :], push, (((1,), (1,)), ((), ())), preferred_element_type=f32
            )
            field_ref[pl.ds(base + 2 + 18 * half, 18)] = part.reshape(18, EXT, NZ)

        def own(x, _):
            field_ref[base + 4 + x, 4:36, :] += velocity_ref[c * CELLS + x]
            return 0

        lax.fori_loop(0, CELLS, own, 0)
        for side, strip in zip(SIDES, strips):
            dx, dy = side
            first, last = (2, 38) if dx == 0 else LOW if dx < 0 else HIGH
            low, high = (0, EXT) if dy == 0 else (0, 8) if dy < 0 else (32, 40)
            part = field_ref[pl.ds(base + first, last - first), low:high, :]
            strip[c] = part.reshape(side_rows(side), NZ).astype(bf16)
        return 0

    lax.fori_loop(0, 3, component, 0)


def spread(received, velocity):
    shapes = [
        jax.ShapeDtypeStruct((3 * EXT, EXT, NZ), f32),
        jax.ShapeDtypeStruct((12 * CAP, 128), f32),
        jax.ShapeDtypeStruct((3 * CAP, 128), i32),
    ] + [jax.ShapeDtypeStruct((3, side_rows(side), NZ), bf16) for side in SIDES]
    return pl.pallas_call(
        spread_kernel,
        out_shape=shapes,
        in_specs=[VMEM, VMEM],
        out_specs=[VMEM] * len(shapes),
        scratch_shapes=[
            pltpu.VMEM((384, 128), f32),
            pltpu.VMEM((ROWS, SLOTS), bf16),
            pltpu.VMEM((3, NZ, SLOTS), bf16),
        ],
        compiler_params=params(56),
        cost_estimate=pl.CostEstimate(flops=2 * ROWS * SLOTS * 3 * NZ, bytes_accessed=10**7, transcendentals=0),
    )(received, velocity)


def laplace(ref, x):
    center = ref[x]
    result = ref[x - 1] + ref[x + 1]
    result = result + pltpu.roll(center, 1, 0) + pltpu.roll(center, EXT - 1, 0)
    result = result + pltpu.roll(center, 1, 1) + pltpu.roll(center, NZ - 1, 1)
    return center + viscosity * (result - 6.0 * center)


def sample_kernel(field_ref, wts_ref, cell_ref, *refs):
    got, (next_ref, out_ref, v0_ref, v1_ref, v2_ref, across_ref, plane_ref, sum_ref) = refs[:8], refs[8:]
    v2_ref[ROWS:, :] = jnp.zeros((1536 - ROWS, NZ), f32)
    plane_ref[ROWS:, :] = jnp.zeros((1536 - ROWS, 256), bf16)

    def component(c, _):
        v0_ref[...] = field_ref[pl.ds(c * EXT, EXT)]
        for side, strip in zip(SIDES, got):
            dx, dy = side
            count = 36 if dx == 0 else 6
            first = 2 if dx == 0 else 34 if dx < 0 else 0
            low, high = (0, EXT) if dy == 0 else (32, 40) if dy < 0 else (0, 8)
            v0_ref[first : first + count, low:high, :] += strip[c].astype(f32).reshape(count, high - low, NZ)

        def first_sweep(x, _):
            v1_ref[x] = laplace(v0_ref, x)
            return 0

        lax.fori_loop(1, EXT - 1, first_sweep, 0)

        def second_sweep(x, _):
            value = laplace(v1_ref, x)
            v2_ref[pl.ds(pl.multiple_of((x - 2) * EXT, 8), EXT), :] = value

            @pl.when((x >= 4) & (x < 36))
            def _():
                next_ref[c * CELLS + x - 4] = value[4:36]

            return 0

        lax.fori_loop(2, EXT - 2, second_sweep, 0)
        for part in range(12):
            piece = v2_ref[128 * part : 128 * part + 128, :]
            across_ref[c, :, 128 * part : 128 * part + 128] = piece.T.astype(bf16)
        return 0

    v1_ref[0] = jnp.zeros((EXT, NZ), f32)
    v1_ref[EXT - 1] = jnp.zeros((EXT, NZ), f32)
    lax.fori_loop(0, 3, component, 0)

    def interpolate(block, _):
        def store(row, both):
            plane_ref[row : row + 80, :] = both

        plane_rows(wts_ref, cell_ref, block, store)
        depth = table(wts_ref, cell_ref, 2, block, NZ)
        for c in range(3):
            mixed = jnp.dot(across_ref[c], plane_ref[...], preferred_element_type=f32)
            total = jnp.sum(mixed * depth, axis=0, keepdims=True)
            sum_ref[pl.ds(64 * c + 2 * block, 1), :] = total[:, :128]
            sum_ref[pl.ds(64 * c + 2 * block + 1, 1), :] = total[:, 128:]
        return 0

    sum_ref[...] = jnp.zeros((256, 128), f32)
    lax.fori_loop(0, BLOCKS, interpolate, 0)
    out_ref[pl.ds(0, 128, stride=2), :] = sum_ref[0:128, :].T
    out_ref[pl.ds(1, 128, stride=2), :] = sum_ref[128:256, :].T


def sample(field, wts, cells, got):
    return pl.pallas_call(
        sample_kernel,
        out_shape=[
            jax.ShapeDtypeStruct((3 * CELLS, CELLS, NZ), f32),
            jax.ShapeDtypeStruct((256, 128), f32),
        ],
        in_specs=[VMEM] * 11,
        out_specs=[VMEM] * 2,
        scratch_shapes=[
            pltpu.VMEM((EXT, EXT, NZ), f32),
            pltpu.VMEM((EXT, EXT, NZ), f32),
            pltpu.VMEM((1536, NZ), f32),
            pltpu.VMEM((3, NZ, 1536), bf16),
            pltpu.VMEM((1536, 256), bf16),
            pltpu.VMEM((256, 128), f32),
        ],
        compiler_params=params(48),
        cost_estimate=pl.CostEstimate(flops=2 * 1536 * SLOTS * 3 * NZ, bytes_accessed=10**7, transcendentals=0),
    )(field, wts, cells, *got)


def unpack_kernel(back_ref, counts_ref, out_ref, flat_ref):
    lane = lax.broadcasted_iota(i32, (16, 128), 1)
    for c in range(3):
        base = 64 * (c % 2)
        rows = [jnp.zeros((16, 128), f32)] * 3
        for j in range(8):
            row0, lane0 = divmod(CAP * j, 128)
            part = back_ref[pl.ds(2 * j + c // 2, 16, stride=16), :]
            part = jnp.where(lane - base < counts_ref[pl.ds(j, 16, stride=8), :], part, 0.0)
            shift = (lane0 - base) % 128
            part = pltpu.roll(part, shift, 1) if shift else part
            rows[row0] = jnp.where((lane >= lane0) & (lane < lane0 + CAP), part, rows[row0])
            if lane0 + CAP > 128:
                rows[row0 + 1] = jnp.where(lane < lane0 + CAP - 128, part, rows[row0 + 1])
        for r in range(3):
            flat_ref[pl.ds(c * CAP + r, 16, stride=3), :] = rows[r]
        for r in range(CAP):
            out_ref[c : c + 1, 128 * r : 128 * r + 128] = flat_ref[c * CAP + r : c * CAP + r + 1, :]


def body(velocity, fiber_loads, fractions, corners, neighbours, counts):
    counts = counts.reshape(DEVICES, 1)
    payload = pl.pallas_call(
        prep_kernel,
        out_shape=jax.ShapeDtypeStruct((4 * DEVICES, 128), f32),
        in_specs=[VMEM] * 5,
        out_specs=VMEM,
        scratch_shapes=[pltpu.VMEM((CAP, 128), f32), pltpu.VMEM((6 * CAP, 128), f32)],
        compiler_params=params(),
    )(fiber_loads, fractions, corners, neighbours.reshape(CAP, 128), counts)
    received = exchange(payload, "gx", GX, "gy", GY, 4, 0).reshape(4 * DEVICES, 128)
    mine = velocity.transpose(2, 0, 1, 3).reshape(3 * CELLS, CELLS, NZ)
    field, wts, cells, *strips = spread(received, mine)
    got = halo_exchange(strips)
    following, samples = sample(field, wts, cells, got)
    back = exchange(samples, "gy", GY, "gx", GX, 2, 2).reshape(2 * DEVICES, 128)
    fiber_velocity = pl.pallas_call(
        unpack_kernel,
        out_shape=jax.ShapeDtypeStruct((3, SLOTS), f32),
        in_specs=[VMEM] * 2,
        out_specs=VMEM,
        scratch_shapes=[pltpu.VMEM((3 * CAP, 128), f32)],
        compiler_params=params(),
    )(back, counts)
    velocity_next = following.reshape(3, CELLS, CELLS, NZ).transpose(1, 2, 0, 3)
    return (velocity_next, fiber_velocity)


def solution(mesh):
    return jax.shard_map(
        body,
        mesh=mesh,
        in_specs=(
            P("gx", "gy", None, None),
            P(None, ("gx", "gy")),
            P(None, ("gx", "gy")),
            P(None, ("gx", "gy")),
            P(("gx", "gy")),
            P(("gx", "gy")),
        ),
        out_specs=(P("gx", "gy", None, None), P(None, ("gx", "gy"))),
        check_vma=False,
    )
```

profile of v0, /device:TPU:1, one launch (start us, length us, event | category | flops | bytes accessed | tf_op | source)
XLA Modules:
  0.0 149.6 jit_solution(1654805836305781018)
XLA Ops:
  0.6 0.8 copy.8.counts_ref
  1.4 0.0 copy-start.5
  1.4 0.9 copy-done.5
  2.3 0.9 copy-done.6
  3.2 0.0 copy-start.7
  3.2 0.9 copy-done.7
  4.1 0.0 copy-start.12
  4.1 0.7 copy-done.12
  4.8 2.8 %shard_map.77 = f32[512,128]{1,0:T(8,128)S(1)} custom-call(f32[3,6144]{1,0:T(4,128)S(1)} %copy-done.5, f32[3,6144]{1,0:T(4,128)S(1)} %copy-done.6, s32[3,6144]{1,0:T(4,128)S(1)} %copy-done.7, s32[48,128]{1,0:T(8,128)S(1)} %bitcast.17, s32[128,1]{1,0:T(8,128)S(1)} %copy.8.counts_ref), custom_call_target="tpu_custom_call" | custom-call | tf_op jit(solution)/shard_map/pallas_call | solution.py:412
  7.6 18.8 %shard_map.78 = f32[16,8,4,128]{3,2,1,0:T(4,128)S(1)} custom-call(f32[8,16,4,128]{3,2,1,0:T(4,128)S(1)} %bitcast.13), custom_call_target="tpu_custom_call" | custom-call | tf_op jit(solution)/shard_map/pallas_call | solution.py:139
  26.4 0.0 copy-start.4
  26.4 0.7 copy-done.4
  27.1 4.0 %copy.9 = f32[3,32,32,256]{3,2,1,0:T(8,128)} copy(f32[3,32,32,256]{3,2,0,1:T(8,128)} %bitcast.18) | data formatting | bytes 6291456 | tf_op jit(solution)/shard_map/transpose | solution.py:421
  31.1 27.1 %shard_map.79 = (f32[120,40,256]{2,1,0:T(8,128)}, f32[576,128]{1,0:T(8,128)}, s32[144,128]{1,0:T(8,128)}, bf16[3,240,256]{2,1,0:T(8,128)(2,1)}, bf16[3,240,256]{...) custom-call(f32[512,128]{1,0:T(8,128)} %bitcast.15, ...), custom_call_target="tpu_custom_call" | custom-call | flops 13589544960 | bytes 10000000 | tf_op jit(solution)/shard_map/pallas_call | solution.py:286
  58.2 0.0 copy-start
  58.2 1.0 copy-done
  59.2 0.0 copy-start.1
  59.2 1.0 copy-done.1
  60.2 1.0 copy-done.2
  61.2 1.0 copy-done.3
  62.2 0.9 copy-done.8
  63.1 0.9 copy-done.9
  64.0 0.9 copy-done.10
  64.9 0.9 copy-done.11
  65.8 19.9 %shard_map.80 = (bf16[3,240,256]{2,1,0:T(8,128)(2,1)S(1)}, bf16[3,240,256]{2,1,0:T(8,128)(2,1)S(1)}, bf16[3,288,256]{2,1,0:T(8,128)(2,1)S(1)}, bf16[3,288,256]{2...) custom-call(bf16[3,240,256]{2,1,0:T(8,128)(2,1)S(1)} %copy-done.2, ...), custom_call_target="tpu_custom_call" | custom-call | tf_op jit(solution)/shard_map/pallas_call | solution.py:189
  85.7 0.0 copy-start.13
  85.7 1.0 copy-done.13
  86.6 0.9 copy-done.14
  87.5 46.0 %shard_map.81 = (f32[96,32,256]{2,1,0:T(8,128)S(1)}, f32[256,128]{1,0:T(8,128)S(1)}) custom-call(f32[120,40,256]{2,1,0:T(8,128)} %get-tuple-element.23.field_ref, f32[576,128]{1,0:T(8,128)S(1)} %copy-done.13, s32[144,128]{1,0:T(8,128)S(1)} %copy-done.14, bf16[3,240,256]{2,1,0:T(8,128)(2,1)S(1)} %get-tuple-element.34.refs_0_, ...), custom_call_target="tpu_custom_call" | custom-call | flops 14495514624 | bytes 10000000 | tf_op jit(solution)/shard_map/pallas_call | solution.py:369
  133.6 2.0 %copy.13 = f32[3,32,32,256]{3,2,0,1:T(8,128)} copy(f32[3,32,32,256]{3,2,1,0:T(8,128)S(1)} %bitcast.12) | data formatting | bytes 6291456 | tf_op jit(solution)/shard_map/reshape | solution.py:434
  135.6 13.1 %shard_map.82 = f32[8,16,2,128]{3,2,1,0:T(2,128)S(1)} custom-call(f32[16,8,2,128]{3,2,1,0:T(2,128)S(1)} %bitcast.16), custom_call_target="tpu_custom_call" | custom-call | tf_op jit(solution)/shard_map/pallas_call | solution.py:139
  148.7 0.9 shard_map.83
  (8 shorter events, 0.0 us)
Async XLA Ops:
  1.4 0.9 copy-start.5
  2.3 0.9 copy-start.6
  3.2 0.9 copy-start.7
  4.1 0.7 copy-start.12
  26.4 0.7 copy-start.4
  58.2 1.0 copy-start
  59.2 1.0 copy-start.1
  60.2 1.0 copy-start.2
  61.2 1.0 copy-start.3
  62.2 0.9 copy-start.8
  63.1 0.9 copy-start.9
  64.0 0.9 copy-start.10
  64.9 0.9 copy-start.11
  85.7 1.0 copy-start.13
  86.6 0.9 copy-start.14
where the time goes:
time: 150 us
  Pallas kernels  129 us (86%)
  local copies, waits for them, and re-layouts  20.3 us (14%)
    pallas_call x1, Pallas kernels, sample(): pl.pallas_call(sample_kernel, out_shape=[jax.ShapeDtypeStruct((3 * CELLS,...  46 us
    pallas_call x2, Pallas kernels, exchange(): pl.pallas_call(kernel, out_shape=jax.ShapeDtypeStruct((second, first, row...  31.9 us
    pallas_call x1, Pallas kernels, spread(): pl.pallas_call(spread_kernel, out_shape=shapes, in_specs=[VMEM, VMEM], ou...  27.1 us
    pallas_call x1, Pallas kernels, halo_exchange(): pl.pallas_call(halo_kernel, out_shape=[jax.ShapeDtypeStruct(s.shape, s.dt...  19.9 us
    unnamed x30, local copies, waits for them, and re-layouts  13.5 us
    transpose x1, local copies, waits for them, and re-layouts, body(): mine = velocity.transpose(2, 0, 1, 3).reshape(3 * CELLS, CELLS, NZ)  3.97 us

commit v1 on v0

v1 whole, which is shorter than its diff:
```python
import functools

import jax
import jax.numpy as jnp
from jax import lax
from jax.experimental import pallas as pl
from jax.experimental.pallas import tpu as pltpu
from jax.sharding import PartitionSpec as P

viscosity = 0.15
GX, GY = 8, 16
DEVICES = GX * GY
CAP = 48
SLOTS = CAP * DEVICES
CELLS = 32
NZ = 256
EXT = 40
ROWS = 36 * EXT
PADDED = 1536
BLOCKS = CAP // 2
MESH = pl.DeviceIdType.MESH
VMEM = pl.BlockSpec(memory_space=pltpu.VMEM)
ANY = pl.BlockSpec(memory_space=pl.ANY)
f32, bf16, i32 = jnp.float32, jnp.bfloat16, jnp.int32


def params(mib=16, **more):
    return pltpu.CompilerParams(vmem_limit_bytes=mib * 2**20, **more)


def fetch(pairs, sems):
    copies = [pltpu.make_async_copy(src, dst, sems.at[k]) for k, (src, dst) in enumerate(pairs)]
    for copy in copies:
        copy.start()
    for copy in copies:
        copy.wait()


def counts_column(counts_ref):
    return jnp.broadcast_to(counts_ref[...].astype(f32), (DEVICES, DEVICES)).T.astype(i32)


def prep_kernel(loads_hbm, frac_hbm, corner_hbm, partner_hbm, counts_hbm, out_ref, *scratch):
    loads_ref, frac_ref, corner_ref, partner_ref, counts_ref, sems, live_ref, flat_ref, pos_ref = scratch
    fetch(
        [
            (loads_hbm, loads_ref),
            (frac_hbm, frac_ref),
            (corner_hbm, corner_ref),
            (partner_hbm, partner_ref),
            (counts_hbm, counts_ref),
        ],
        sems,
    )
    live_ref[...] = counts_column(counts_ref)

    def flat_rows(ref, c):
        for r in range(CAP):
            flat_ref[r : r + 1, :] = ref[c : c + 1, 128 * r : 128 * r + 128].astype(f32)
        return flat_ref[...]

    lane = lax.broadcasted_iota(i32, (CAP, 128), 1)
    flat_id = lax.broadcasted_iota(i32, (CAP, 128), 0) * 128 + lane
    bucket = (flat_id * 43691) >> 21
    partner = partner_ref[...]
    high, low = partner >> 7, partner & 127
    whole = (CELLS * GX, CELLS * GY, NZ)
    for c in range(3):
        fraction = flat_rows(frac_ref, c)
        corner = flat_rows(corner_ref, c)
        loads = flat_rows(loads_ref, c)
        position = corner + fraction
        flat_ref[...] = position
        gathered = jnp.zeros((CAP, 128), f32)
        for r in range(CAP):
            row = jnp.broadcast_to(flat_ref[r : r + 1, :], (CAP, 128))
            taken = jnp.take_along_axis(row, low, axis=1, mode="promise_in_bounds")
            gathered = jnp.where(high == r, taken, gathered)
        forcing = loads + (2.0 / whole[c]) * (gathered - position)
        pos_ref[c * CAP : c * CAP + CAP, :] = forcing
        cell = corner.astype(i32)
        if c == 0:
            cell = (cell - (bucket >> 4) * CELLS + 4) & (whole[0] - 1)
        if c == 1:
            cell = (cell - (bucket & 15) * CELLS + 4) & (whole[1] - 1)
        pos_ref[(3 + c) * CAP : (3 + c) * CAP + CAP, :] = cell.astype(f32) + fraction

    lane = lax.broadcasted_iota(i32, (16, 128), 1)
    for j in range(8):
        row0, lane0 = divmod(CAP * j, 128)
        live = (lane & 63) < live_ref[pl.ds(j, 16, stride=8), :]

        def piece(v, target):
            part = pos_ref[pl.ds(v * CAP + row0, 16, stride=3), :]
            if lane0 + CAP > 128:
                later = pos_ref[pl.ds(v * CAP + row0 + 1, 16, stride=3), :]
                part = jnp.where(lane >= lane0, part, later)
            shift = (target - lane0) % 128
            return pltpu.roll(part, shift, 1) if shift else part

        for pair in range(3):
            row = jnp.where(lane < 64, piece(2 * pair, 0), piece(2 * pair + 1, 64))
            if pair == 0:
                row = jnp.where(live, row, 0.0)
            if pair == 1:
                row = jnp.where(live | (lane >= 64), row, 0.0)
            out_ref[pl.ds(4 * j + pair, 16, stride=32), :] = row
        out_ref[pl.ds(4 * j + 3, 16, stride=32), :] = jnp.zeros((16, 128), f32)


def send(src, dst, sems, at, peer):
    copy = pltpu.make_async_remote_copy(
        src_ref=src,
        dst_ref=dst,
        send_sem=sems[0].at[at],
        recv_sem=sems[1].at[at],
        device_id=peer,
        device_id_type=MESH,
    )
    copy.start()
    return copy


def two_stage(first_axis, first, second_axis, second, x_ref, mid_ref, out_ref, sems1, sems2, here):
    me1, me2 = lax.axis_index(first_axis), lax.axis_index(second_axis)
    own = pltpu.make_async_copy(x_ref.at[me1], mid_ref.at[me1], here.at[0])
    copies = []
    for k in range(1, first):
        peer = lax.rem(me1 + k, first)
        copies.append(send(x_ref.at[peer], mid_ref.at[me1], sems1, k, {first_axis: peer}))
    own.start()
    own.wait()
    for copy in copies:
        copy.wait_recv()
    own = pltpu.make_async_copy(mid_ref.at[:, me2], out_ref.at[me2], here.at[1])
    later = []
    for k in range(1, second):
        peer = lax.rem(me2 + k, second)
        later.append(send(mid_ref.at[:, peer], out_ref.at[me2], sems2, k, {second_axis: peer}))
    own.start()
    own.wait()
    for copy in later:
        copy.wait_recv()
    for copy in copies + later:
        copy.wait_send()


SIDES = ((-1, 0), (1, 0), (0, -1), (0, 1), (-1, -1), (-1, 1), (1, -1), (1, 1))
LOW, HIGH = (2, 8), (32, 38)


def side_rows(side):
    dx, dy = side
    return 6 * EXT if dy == 0 else 36 * 8 if dx == 0 else 6 * 8


def point_row(ref, base, block):
    return jnp.concatenate([ref[pl.ds(base + 2 * block, 1), :], ref[pl.ds(base + 2 * block + 1, 1), :]], axis=1)


def table(wts_ref, cell_ref, dim, block, length):
    corner = point_row(cell_ref, dim * CAP, block)
    delta = lax.broadcasted_iota(i32, (length, 256), 0) - corner
    if dim == 2:
        delta = delta & (NZ - 1)
    result = jnp.zeros((length, 256), f32)
    for k in range(4):
        result = jnp.where(delta == k, point_row(wts_ref, (4 * dim + k) * CAP, block), result)
    return result


def weights(values_ref, wts_ref, cell_ref):
    for dim in range(3):
        position = values_ref[64 * (3 + dim) : 64 * (3 + dim) + CAP, :]
        corner = jnp.floor(position)
        angle = (0.5 * jnp.pi) * (position - corner)
        sine, cosine = jnp.sin(angle), jnp.cos(angle)
        cell_ref[dim * CAP : dim * CAP + CAP, :] = corner.astype(i32)
        for k, term in enumerate((-sine, cosine, sine, -cosine)):
            at = (4 * dim + k) * CAP
            wts_ref[at : at + CAP, :] = 0.25 * (1.0 + term)


def fill_tables(values_ref, wts_ref, cell_ref, plane_ref, push_ref, depth_ref):
    def fill(block, _):
        columns = pl.ds(pl.multiple_of(block * 256, 256), 256)
        along_x = table(wts_ref, cell_ref, 0, block, EXT)
        along_y = table(wts_ref, cell_ref, 1, block, EXT)
        for i in range(18):
            x = 2 + 2 * i
            both = jnp.concatenate([along_y * along_x[x : x + 1], along_y * along_x[x + 1 : x + 2]], axis=0)
            plane_ref[80 * i : 80 * i + 80, columns] = both.astype(bf16)
        depth = table(wts_ref, cell_ref, 2, block, NZ)
        depth_ref[:, columns] = depth
        for c in range(3):
            push_ref[c, :, columns] = (depth * point_row(values_ref, 64 * c, block)).astype(bf16)
        return 0

    plane_ref[ROWS:, :] = jnp.zeros((PADDED - ROWS, SLOTS), bf16)
    lax.fori_loop(0, BLOCKS, fill, 0)


def laplace(ref, x):
    center = ref[x]
    around = ref[x - 1] + ref[x + 1]
    around = around + pltpu.roll(center, 1, 0) + pltpu.roll(center, EXT - 1, 0)
    around = around + pltpu.roll(center, 1, 1) + pltpu.roll(center, NZ - 1, 1)
    return (1.0 - 6.0 * viscosity) * center + viscosity * around


def spread(c, velocity_ref, plane_ref, push_ref, field_ref, strips):
    field = field_ref.at[c]
    empty = jnp.zeros((2, EXT, NZ), f32)
    field[0:2] = empty
    field[38:40] = empty
    for half in range(2):
        part = lax.dot_general(
            plane_ref[720 * half : 720 * half + 720, :],
            push_ref[c],
            (((1,), (1,)), ((), ())),
            preferred_element_type=f32,
        )
        field[2 + 18 * half : 20 + 18 * half] = part.reshape(18, EXT, NZ)

    def own(t, _):
        for k in range(8):
            x = t * 8 + k
            field[4 + x, 4:36, :] += velocity_ref[c * CELLS + x]
        return 0

    lax.fori_loop(0, CELLS // 8, own, 0)
    for side, strip in zip(SIDES, strips):
        dx, dy = side
        first, last = (2, 38) if dx == 0 else LOW if dx < 0 else HIGH
        low, high = (0, EXT) if dy == 0 else (0, 8) if dy < 0 else (32, 40)
        strip[c] = field[first:last, low:high, :].reshape(side_rows(side), NZ).astype(bf16)


def sweep(c, field_ref, got, v1_ref, v2_ref, next_ref, across_ref):
    field = field_ref.at[c]
    for side, strip in zip(SIDES, got):
        dx, dy = side
        count = 36 if dx == 0 else 6
        first = 2 if dx == 0 else 34 if dx < 0 else 0
        low, high = (0, EXT) if dy == 0 else (32, 40) if dy < 0 else (0, 8)
        field[first : first + count, low:high, :] += strip[c].astype(f32).reshape(count, high - low, NZ)

    def first_sweep(t, _):
        for k in range(12):
            x = 1 + t * 12 + k
            v1_ref[x] = laplace(field, x)
        return 0

    lax.fori_loop(0, 3, first_sweep, 0)
    for x in (37, 38):
        v1_ref[x] = laplace(field, x)

    def second(x):
        value = laplace(v1_ref, x)
        v2_ref[pl.ds(pl.multiple_of((x - 2) * EXT, 8), EXT), :] = value
        return value

    for x in (2, 3, 36, 37):
        second(x)

    def second_sweep(t, _):
        for k in range(8):
            x = 4 + t * 8 + k
            next_ref[c * CELLS + x - 4] = second(x)[4:36]
        return 0

    lax.fori_loop(0, 4, second_sweep, 0)
    for part in range(PADDED // 128):
        piece = v2_ref[128 * part : 128 * part + 128, :]
        across_ref[c, :, 128 * part : 128 * part + 128] = piece.T.astype(bf16)


def interpolate(c, across_ref, plane_ref, depth_ref, sum_ref):
    def some(t, _):
        columns = pl.ds(pl.multiple_of(t * 1024, 1024), 1024)
        mixed = jnp.dot(across_ref[c], plane_ref[:, columns], preferred_element_type=f32)
        total = jnp.sum(mixed * depth_ref[:, columns], axis=0, keepdims=True)
        for k in range(8):
            sum_ref[pl.ds(64 * c + 8 * t + k, 1), :] = total[:, 128 * k : 128 * k + 128]
        return 0

    lax.fori_loop(0, SLOTS // 1024, some, 0)


def step_kernel(payload_ref, velocity_ref, next_ref, back_ref, *scratch):
    (
        mid_ref, recv_ref, values_ref, wts_ref, cell_ref, plane_ref, push_ref, depth_ref, field_ref,
        v1_ref, v2_ref, across_ref, sum_ref, send_ref, middle_ref,
    ) = scratch[:15]
    strips, got, sems = scratch[15:23], scratch[23:31], scratch[31:]
    ahead = (sems[0:2], sems[2:4])
    behind = (sems[4:6], sems[6:8])
    around, here = sems[8:10], sems[10]
    gx, gy = lax.axis_index("gx"), lax.axis_index("gy")
    sides = [(lax.rem(gx + dx + GX, GX), lax.rem(gy + dy + GY, GY)) for dx, dy in SIDES]
    peers = [(lax.rem(gx + k, GX), gy) for k in range(1, GX)] + [(gx, lax.rem(gy + k, GY)) for k in range(1, GY)]
    peers = peers + sides[4:]
    barrier = pltpu.get_barrier_semaphore()
    for peer in peers:
        pl.semaphore_signal(barrier, inc=1, device_id=peer, device_id_type=MESH)
    pl.semaphore_wait(barrier, len(peers))

    two_stage("gx", GX, "gy", GY, payload_ref, mid_ref, recv_ref, *ahead, here.at[0:2])
    received = recv_ref[...].reshape(DEVICES, 4, 128)
    for pair in range(3):
        values_ref[128 * pair : 128 * pair + 128, :] = received[:, pair, :].T
    weights(values_ref, wts_ref, cell_ref)
    fill_tables(values_ref, wts_ref, cell_ref, plane_ref, push_ref, depth_ref)
    v1_ref[0] = jnp.zeros((EXT, NZ), f32)
    v1_ref[EXT - 1] = jnp.zeros((EXT, NZ), f32)
    v2_ref[ROWS:, :] = jnp.zeros((PADDED - ROWS, NZ), f32)
    sum_ref[...] = jnp.zeros((256, 128), f32)
    copies = []

    def spread_and_send(c):
        spread(c, velocity_ref, plane_ref, push_ref, field_ref, strips)
        copies.append([send(strips[k].at[c], got[k].at[c], around, 8 * c + k, sides[k]) for k in range(8)])

    def receive_and_sweep(c):
        for copy in copies[c]:
            copy.wait_recv()
        sweep(c, field_ref, got, v1_ref, v2_ref, next_ref, across_ref)

    spread_and_send(0)
    spread_and_send(1)
    receive_and_sweep(0)
    spread_and_send(2)
    receive_and_sweep(1)
    interpolate(0, across_ref, plane_ref, depth_ref, sum_ref)
    receive_and_sweep(2)
    interpolate(1, across_ref, plane_ref, depth_ref, sum_ref)
    interpolate(2, across_ref, plane_ref, depth_ref, sum_ref)
    send_ref[...] = jnp.stack([sum_ref[0:128, :].T, sum_ref[128:256, :].T], axis=1).reshape(GY, GX, 2, 128)
    two_stage("gy", GY, "gx", GX, send_ref, middle_ref, back_ref, *behind, here.at[2:4])
    for some in copies:
        for copy in some:
            copy.wait_send()


def step(payload, velocity):
    dma = pltpu.SemaphoreType.DMA
    strips = [pltpu.VMEM((3, side_rows(side), NZ), bf16) for side in SIDES]
    return pl.pallas_call(
        step_kernel,
        out_shape=[
            jax.ShapeDtypeStruct((3 * CELLS, CELLS, NZ), f32),
            jax.ShapeDtypeStruct((GX, GY, 2, 128), f32),
        ],
        in_specs=[VMEM, VMEM],
        out_specs=[VMEM, VMEM],
        scratch_shapes=[
            pltpu.VMEM((GX, GY, 4, 128), f32),
            pltpu.VMEM((GY, GX, 4, 128), f32),
            pltpu.VMEM((384, 128), f32),
            pltpu.VMEM((12 * CAP, 128), f32),
            pltpu.VMEM((3 * CAP, 128), i32),
            pltpu.VMEM((PADDED, SLOTS), bf16),
            pltpu.VMEM((3, NZ, SLOTS), bf16),
            pltpu.VMEM((NZ, SLOTS), f32),
            pltpu.VMEM((3, EXT, EXT, NZ), f32),
            pltpu.VMEM((EXT, EXT, NZ), f32),
            pltpu.VMEM((PADDED, NZ), f32),
            pltpu.VMEM((3, NZ, PADDED), bf16),
            pltpu.VMEM((256, 128), f32),
            pltpu.VMEM((GY, GX, 2, 128), f32),
            pltpu.VMEM((GY, GX, 2, 128), f32),
            *strips,
            *strips,
            dma((GX,)), dma((GX,)), dma((GY,)), dma((GY,)),
            dma((GY,)), dma((GY,)), dma((GX,)), dma((GX,)),
            dma((24,)), dma((24,)), dma((4,)),
        ],
        compiler_params=params(61, collective_id=0, has_side_effects=True),
        cost_estimate=pl.CostEstimate(flops=4 * PADDED * SLOTS * 3 * NZ, bytes_accessed=10**7, transcendentals=0),
    )(payload, velocity)


def unpack_kernel(back_hbm, counts_hbm, out_ref, back_ref, counts_ref, sems, live_ref, flat_ref):
    fetch([(back_hbm, back_ref), (counts_hbm, counts_ref)], sems)
    live_ref[...] = counts_column(counts_ref)
    lane = lax.broadcasted_iota(i32, (16, 128), 1)
    for c in range(3):
        base = 64 * (c % 2)
        rows = [jnp.zeros((16, 128), f32)] * 3
        for j in range(8):
            row0, lane0 = divmod(CAP * j, 128)
            part = back_ref[pl.ds(2 * j + c // 2, 16, stride=16), :]
            part = jnp.where(lane - base < live_ref[pl.ds(j, 16, stride=8), :], part, 0.0)
            shift = (lane0 - base) % 128
            part = pltpu.roll(part, shift, 1) if shift else part
            rows[row0] = jnp.where((lane >= lane0) & (lane < lane0 + CAP), part, rows[row0])
            if lane0 + CAP > 128:
                rows[row0 + 1] = jnp.where(lane < lane0 + CAP - 128, part, rows[row0 + 1])
        for r in range(3):
            flat_ref[pl.ds(c * CAP + r, 16, stride=3), :] = rows[r]
        for r in range(CAP):
            out_ref[c : c + 1, 128 * r : 128 * r + 128] = flat_ref[c * CAP + r : c * CAP + r + 1, :]


def body(velocity, fiber_loads, fractions, corners, neighbours, counts):
    counts = counts.reshape(1, DEVICES)
    dma = pltpu.SemaphoreType.DMA
    payload = pl.pallas_call(
        prep_kernel,
        out_shape=jax.ShapeDtypeStruct((4 * DEVICES, 128), f32),
        in_specs=[ANY] * 5,
        out_specs=VMEM,
        scratch_shapes=[
            pltpu.VMEM((3, SLOTS), f32),
            pltpu.VMEM((3, SLOTS), f32),
            pltpu.VMEM((3, SLOTS), i32),
            pltpu.VMEM((CAP, 128), i32),
            pltpu.VMEM((1, DEVICES), i32),
            dma((5,)),
            pltpu.VMEM((DEVICES, DEVICES), i32),
            pltpu.VMEM((CAP, 128), f32),
            pltpu.VMEM((6 * CAP, 128), f32),
        ],
        compiler_params=params(),
    )(fiber_loads, fractions, corners, neighbours.reshape(CAP, 128), counts)
    mine = velocity.transpose(2, 0, 1, 3).reshape(3 * CELLS, CELLS, NZ)
    following, back = step(payload.reshape(GX, GY, 4, 128), mine)
    fiber_velocity = pl.pallas_call(
        unpack_kernel,
        out_shape=jax.ShapeDtypeStruct((3, SLOTS), f32),
        in_specs=[ANY] * 2,
        out_specs=VMEM,
        scratch_shapes=[
            pltpu.VMEM((2 * DEVICES, 128), f32),
            pltpu.VMEM((1, DEVICES), i32),
            dma((2,)),
            pltpu.VMEM((DEVICES, DEVICES), i32),
            pltpu.VMEM((3 * CAP, 128), f32),
        ],
        compiler_params=params(),
    )(back.reshape(2 * DEVICES, 128), counts)
    velocity_next = following.reshape(3, CELLS, CELLS, NZ).transpose(1, 2, 0, 3)
    return (velocity_next, fiber_velocity)


def solution(mesh):
    return jax.shard_map(
        body,
        mesh=mesh,
        in_specs=(
            P("gx", "gy", None, None),
            P(None, ("gx", "gy")),
            P(None, ("gx", "gy")),
            P(None, ("gx", "gy")),
            P(("gx", "gy")),
            P(("gx", "gy")),
        ),
        out_specs=(P("gx", "gy", None, None), P(None, ("gx", "gy"))),
        check_vma=False,
    )
```

time: 150 us -> 102 us (0.68)
  Pallas kernels: 129 us -> 88.2 us
  local copies, waits for them, and re-layouts: 20.3 us -> 12.7 us
    pallas_call x5 -> x1, Pallas kernels: 125 us -> 83.8 us  [step(): pl.pallas_call(step_kernel, out_shape=[jax.ShapeDtypeStruct((3 * CELLS, C...]
    unnamed x30 -> x16, local copies, waits for them, and re-layouts: 13.5 us -> 4.77 us
    reshape x1, local copies, waits for them, and re-layouts: 2.04 us -> 4 us  [body(): velocity_next = following.reshape(3, CELLS, CELLS, NZ).transpose(1, 2, 0, 3)]
where the time goes in v1:
time: 102 us
  Pallas kernels  88.2 us (86%)
  local copies, waits for them, and re-layouts  12.7 us (12%)
    pallas_call x1, Pallas kernels, step(): pl.pallas_call(step_kernel, out_shape=[jax.ShapeDtypeStruct((3 * CELLS, C...  83.8 us
    unnamed x16, local copies, waits for them, and re-layouts  4.77 us
    reshape x1, local copies, waits for them, and re-layouts, body(): velocity_next = following.reshape(3, CELLS, CELLS, NZ).transpose(1, 2, 0, 3)  4 us
    transpose x1, local copies, waits for them, and re-layouts, body(): mine = velocity.transpose(2, 0, 1, 3).reshape(3 * CELLS, CELLS, NZ)  3.97 us
    pallas_call x1, Pallas kernels, body(): pl.pallas_call(prep_kernel, out_shape=jax.ShapeDtypeStruct((4 * DEVICES,...  3.3 us

profile of v1, /device:TPU:1, one launch (start us, length us, event | category | flops | bytes accessed | tf_op | source)
XLA Modules:
  0.0 101.8 jit_solution(5965310925352535689)
XLA Ops:
  0.6 0.0 copy-start.2
  0.6 0.9 copy-done.2
  1.5 0.0 copy-start.3
  1.5 0.9 copy-done.3
  2.4 0.0 copy-start.4
  2.4 0.9 copy-done.4
  3.3 0.0 copy-start.5
  3.3 0.7 copy-done.5
  4.0 0.0 copy-start.6
  4.1 0.7 copy-done.6
  4.7 3.3 %shard_map.77 = f32[512,128]{1,0:T(8,128)S(1)} custom-call(f32[3,6144]{1,0:T(4,128)S(1)} %copy-done.2, f32[3,6144]{1,0:T(4,128)S(1)} %copy-done.3, s32[3,6144]{1,0:T(4,128)S(1)} %copy-done.4, s32[48,128]{1,0:T(8,128)S(1)} %bitcast.12, s32[1,128]{1,0:T(1,128)S(1)} %bitcast.13), custom_call_target="tpu_custom_call" | custom-call | tf_op jit(solution)/shard_map/pallas_call | solution.py:408
  8.0 0.0 copy-start
  8.0 0.7 copy-done
  8.7 4.0 %copy.8 = f32[3,32,32,256]{3,2,1,0:T(8,128)} copy(f32[3,32,32,256]{3,2,0,1:T(8,128)} %bitcast.15) | data formatting | bytes 6291456 | tf_op jit(solution)/shard_map/transpose | solution.py:426
  12.7 83.8 %shard_map.78 = (f32[96,32,256]{2,1,0:T(8,128)}, f32[8,16,2,128]{3,2,1,0:T(2,128)}) custom-call(f32[8,16,4,128]{3,2,1,0:T(4,128)} %bitcast.10, f32[96,32,256]{2,1,0:T(8,128)} %bitcast.18), custom_call_target="tpu_custom_call" | custom-call | flops 28991029248 | bytes 10000000 | tf_op jit(solution)/shard_map/pallas_call | solution.py:348
  96.5 0.0 copy-start.1
  96.6 0.0 copy-start.7
  96.6 4.0 %copy.11 = f32[3,32,32,256]{3,2,0,1:T(8,128)} copy(f32[3,32,32,256]{3,2,1,0:T(8,128)} %bitcast.17) | data formatting | bytes 6291456 | tf_op jit(solution)/shard_map/reshape | solution.py:442
  100.6 0.0 copy-done.1
  100.6 0.0 copy-done.7
  100.6 1.1 %shard_map.79 = f32[3,6144]{1,0:T(4,128)} custom-call(f32[256,128]{1,0:T(8,128)S(1)} %bitcast.11, s32[1,128]{1,0:T(1,128)S(1)} %bitcast.14), custom_call_target="tpu_custom_call" | custom-call | tf_op jit(solution)/shard_map/pallas_call | solution.py:428
Async XLA Ops:
  0.6 0.9 copy-start.2
  1.5 0.9 copy-start.3
  2.4 0.9 copy-start.4
  3.3 0.7 copy-start.5
  4.0 0.7 copy-start.6
  8.0 0.7 copy-start
  96.5 4.0 %copy-start.1 = (f32[8,16,2,128]{3,2,1,0:T(2,128)S(1)}, f32[8,16,2,128]{3,2,1,0:T(2,128)}, u32[]{:S(2)}) copy-start(f32[8,16,2,128]{3,2,1,0:T(2,128)} %get-tuple-element.5) | copy-start | bytes 393220
  96.6 4.0 %copy-start.7 = (s32[128]{0:T(128)S(1)}, s32[128]{0:T(128)}, u32[]{:S(2)}) copy-start(s32[128]{0:T(128)} %param.11) | copy-start | bytes 1540

commit v2 on v1

v2 whole, which is shorter than its diff:
```python
import functools

import jax
import jax.numpy as jnp
from jax import lax
from jax.experimental import pallas as pl
from jax.experimental.pallas import tpu as pltpu
from jax.sharding import PartitionSpec as P

viscosity = 0.15
GX, GY = 8, 16
DEVICES = GX * GY
CAP = 48
SLOTS = CAP * DEVICES
CELLS = 32
NZ = 256
EXT = 40
ROWS = 36 * EXT
PADDED = 1536
BLOCKS = CAP // 2
MESH = pl.DeviceIdType.MESH
VMEM = pl.BlockSpec(memory_space=pltpu.VMEM)
ANY = pl.BlockSpec(memory_space=pl.ANY)
f32, bf16, i32 = jnp.float32, jnp.bfloat16, jnp.int32


def params(mib=16, **more):
    return pltpu.CompilerParams(vmem_limit_bytes=mib * 2**20, **more)


def fetch(pairs, sems):
    copies = [pltpu.make_async_copy(src, dst, sems.at[k]) for k, (src, dst) in enumerate(pairs)]
    for copy in copies:
        copy.start()
    for copy in copies:
        copy.wait()


def counts_column(counts_ref):
    return jnp.broadcast_to(counts_ref[...].astype(f32), (DEVICES, DEVICES)).T.astype(i32)


def prepare(loads_ref, frac_ref, corner_ref, partner_ref, counts_ref, live_ref, flat_ref, pos_ref, out_ref):
    live_ref[...] = counts_column(counts_ref)

    def flat_rows(ref, c):
        for r in range(CAP):
            flat_ref[r : r + 1, :] = ref[c : c + 1, 128 * r : 128 * r + 128].astype(f32)
        return flat_ref[...]

    lane = lax.broadcasted_iota(i32, (CAP, 128), 1)
    flat_id = lax.broadcasted_iota(i32, (CAP, 128), 0) * 128 + lane
    bucket = (flat_id * 43691) >> 21
    partner = partner_ref[...]
    high, low = partner >> 7, partner & 127
    whole = (CELLS * GX, CELLS * GY, NZ)
    for c in range(3):
        fraction = flat_rows(frac_ref, c)
        corner = flat_rows(corner_ref, c)
        loads = flat_rows(loads_ref, c)
        position = corner + fraction
        flat_ref[...] = position
        gathered = jnp.zeros((CAP, 128), f32)
        for r in range(CAP):
            row = jnp.broadcast_to(flat_ref[r : r + 1, :], (CAP, 128))
            taken = jnp.take_along_axis(row, low, axis=1, mode="promise_in_bounds")
            gathered = jnp.where(high == r, taken, gathered)
        forcing = loads + (2.0 / whole[c]) * (gathered - position)
        pos_ref[c * CAP : c * CAP + CAP, :] = forcing
        cell = corner.astype(i32)
        if c == 0:
            cell = (cell - (bucket >> 4) * CELLS + 4) & (whole[0] - 1)
        if c == 1:
            cell = (cell - (bucket & 15) * CELLS + 4) & (whole[1] - 1)
        pos_ref[(3 + c) * CAP : (3 + c) * CAP + CAP, :] = cell.astype(f32) + fraction

    lane = lax.broadcasted_iota(i32, (8, 128), 1)
    for j in range(16):
        row0, lane0 = divmod(CAP * j, 128)
        live = (lane & 63) < live_ref[pl.ds(j, 8, stride=16), :]

        def piece(v, target):
            part = pos_ref[pl.ds(v * CAP + row0, 8, stride=6), :]
            if lane0 + CAP > 128:
                later = pos_ref[pl.ds(v * CAP + row0 + 1, 8, stride=6), :]
                part = jnp.where(lane >= lane0, part, later)
            shift = (target - lane0) % 128
            return pltpu.roll(part, shift, 1) if shift else part

        for pair in range(3):
            row = jnp.where(lane < 64, piece(2 * pair, 0), piece(2 * pair + 1, 64))
            if pair == 0:
                row = jnp.where(live, row, 0.0)
            if pair == 1:
                row = jnp.where(live | (lane >= 64), row, 0.0)
            out_ref[pl.ds(16 * pair + j, 8, stride=48), :] = row


def send(src, dst, sems, at, peer):
    copy = pltpu.make_async_remote_copy(
        src_ref=src,
        dst_ref=dst,
        send_sem=sems[0].at[at],
        recv_sem=sems[1].at[at],
        device_id=peer,
        device_id_type=MESH,
    )
    copy.start()
    return copy


def first_stage(axis, count, x_ref, mid_ref, sems, here):
    me = lax.axis_index(axis)
    own = pltpu.make_async_copy(x_ref.at[me], mid_ref.at[me], here)
    copies = []
    for k in range(1, count):
        peer = lax.rem(me + k, count)
        copies.append(send(x_ref.at[peer], mid_ref.at[me], sems, k, {axis: peer}))
    own.start()
    return [own], copies


def received(stage):
    own, copies = stage
    own[0].wait()
    for copy in copies:
        copy.wait_recv()


def sent(stage):
    for copy in stage[1]:
        copy.wait_send()


SIDES = ((-1, 0), (1, 0), (0, -1), (0, 1), (-1, -1), (-1, 1), (1, -1), (1, 1))
LOW, HIGH = (2, 8), (32, 38)


def side_rows(side):
    dx, dy = side
    return 6 * EXT if dy == 0 else 36 * 8 if dx == 0 else 6 * 8


def point_row(ref, base, block):
    return jnp.concatenate([ref[pl.ds(base + 2 * block, 1), :], ref[pl.ds(base + 2 * block + 1, 1), :]], axis=1)


def table(wts_ref, cell_ref, dim, block, length):
    corner = point_row(cell_ref, dim * CAP, block)
    delta = lax.broadcasted_iota(i32, (length, 256), 0) - corner
    if dim == 2:
        delta = delta & (NZ - 1)
    result = jnp.zeros((length, 256), f32)
    for k in range(4):
        result = jnp.where(delta == k, point_row(wts_ref, (4 * dim + k) * CAP, block), result)
    return result


def weights(values_ref, wts_ref, cell_ref):
    for dim in range(3):
        position = values_ref[64 * (3 + dim) : 64 * (3 + dim) + CAP, :]
        corner = jnp.floor(position)
        angle = (0.5 * jnp.pi) * (position - corner)
        sine, cosine = jnp.sin(angle), jnp.cos(angle)
        cell_ref[dim * CAP : dim * CAP + CAP, :] = corner.astype(i32)
        for k, term in enumerate((-sine, cosine, sine, -cosine)):
            at = (4 * dim + k) * CAP
            wts_ref[at : at + CAP, :] = 0.25 * (1.0 + term)


def fill_tables(values_ref, wts_ref, cell_ref, plane_ref, push_ref, depth_ref):
    def fill(block, _):
        columns = pl.ds(pl.multiple_of(block * 256, 256), 256)
        along_x = table(wts_ref, cell_ref, 0, block, EXT)
        along_y = table(wts_ref, cell_ref, 1, block, EXT)
        for i in range(18):
            x = 2 + 2 * i
            both = jnp.concatenate([along_y * along_x[x : x + 1], along_y * along_x[x + 1 : x + 2]], axis=0)
            plane_ref[80 * i : 80 * i + 80, columns] = both.astype(bf16)
        depth = table(wts_ref, cell_ref, 2, block, NZ)
        depth_ref[:, columns] = depth
        for c in range(3):
            push_ref[c, :, columns] = (depth * point_row(values_ref, 64 * c, block)).astype(bf16)
        return 0

    lax.fori_loop(0, BLOCKS, fill, 0)


def laplace(ref, x):
    center = ref[x]
    around = ref[x - 1] + ref[x + 1]
    around = around + pltpu.roll(center, 1, 0) + pltpu.roll(center, EXT - 1, 0)
    around = around + pltpu.roll(center, 1, 1) + pltpu.roll(center, NZ - 1, 1)
    return (1.0 - 6.0 * viscosity) * center + viscosity * around


def place_velocity(velocity_ref, field_ref):
    def place(t, _):
        for k in range(4):
            x = 4 * t + k
            for c in range(3):
                field_ref[c, x] = jnp.zeros((EXT, NZ), f32)
        return 0

    lax.fori_loop(0, EXT // 4, place, 0)

    def own(t, _):
        for k in range(4):
            x = 4 * t + k
            for c in range(3):
                field_ref[c, 4 + x, 4:36, :] = velocity_ref[x, c]
        return 0

    lax.fori_loop(0, CELLS // 4, own, 0)


def side_range(side):
    dx, dy = side
    first, last = (2, 38) if dx == 0 else LOW if dx < 0 else HIGH
    low, high = (0, EXT) if dy == 0 else (0, 8) if dy < 0 else (32, 40)
    return first, last, low, high


def opposite_range(side):
    dx, dy = side
    first, last = (2, 38) if dx == 0 else (34, 40) if dx < 0 else (0, 6)
    low, high = (0, EXT) if dy == 0 else (32, 40) if dy < 0 else (0, 8)
    return first, last, low, high


def pass_over(tasks):
    def some(t, _):
        for task in tasks:
            task(t)
        return 0

    lax.fori_loop(0, 6, some, 0)


def step_kernel(*refs):
    inputs, velocity_hbm = refs[:5], refs[5]
    next_hbm, back_ref = refs[6:8]
    scratch = refs[8:]
    staged, fetch_sems, (live_ref, flat_ref, pos_ref, payload_ref) = scratch[:5], scratch[5], scratch[6:10]
    mid_ref, turned_ref, recv_ref, values_ref, wts_ref, cell_ref = scratch[10:16]
    plane_ref, push_ref, depth_ref, field_ref, v1_ref, v2_ref, across_ref = scratch[16:23]
    sum_ref, out_ref, middle_ref, about_ref, velocity_ref, next_ref = scratch[23:29]
    strips, got, sems = scratch[29:37], scratch[37:45], scratch[45:]
    ahead, behind, around = (sems[0:2], sems[2:4]), (sems[4:6], sems[6:8], sems[8:10], sems[10:12]), sems[12:14]
    here, bulk = sems[14], sems[15]

    gx, gy = lax.axis_index("gx"), lax.axis_index("gy")
    sides = [(lax.rem(gx + dx + GX, GX), lax.rem(gy + dy + GY, GY)) for dx, dy in SIDES]
    peers = [(lax.rem(gx + k, GX), gy) for k in range(1, GX)] + [(gx, lax.rem(gy + k, GY)) for k in range(1, GY)]
    peers = peers + sides[4:]
    barrier = pltpu.get_barrier_semaphore()
    for peer in peers:
        pl.semaphore_signal(barrier, inc=1, device_id=peer, device_id_type=MESH)
    fetch(list(zip(inputs, staged)), fetch_sems)
    own_velocity = pltpu.make_async_copy(velocity_hbm, velocity_ref, bulk.at[3])
    own_velocity.start()
    prepare(*staged, live_ref, flat_ref, pos_ref, payload_ref)
    pl.semaphore_wait(barrier, len(peers))

    stage1 = first_stage("gx", GX, payload_ref.reshape(GX, 48, 128), mid_ref, ahead[0], here.at[0])
    own_velocity.wait()
    place_velocity(velocity_ref, field_ref)
    received(stage1)
    for a in range(GX):
        for pair in range(3):
            turned_ref[pl.ds(8 * pair + a, GY, stride=24), :] = mid_ref[a, 16 * pair : 16 * pair + 16, :]
    stage2 = first_stage("gy", GY, turned_ref.reshape(GY, 24, 128), recv_ref, ahead[1], here.at[1])
    plane_ref[ROWS:, :] = jnp.zeros((PADDED - ROWS, SLOTS), bf16)
    v2_ref[ROWS:, :] = jnp.zeros((PADDED - ROWS, NZ), f32)
    sum_ref[...] = jnp.zeros((256, 128), f32)
    received(stage2)
    for pair in range(3):
        values_ref[128 * pair : 128 * pair + 128, :] = recv_ref[:, 8 * pair : 8 * pair + 8, :].reshape(DEVICES, 128).T
    weights(values_ref, wts_ref, cell_ref)
    fill_tables(values_ref, wts_ref, cell_ref, plane_ref, push_ref, depth_ref)

    def spread(c):
        def some(t):
            part = lax.dot_general(
                plane_ref[pl.ds(pl.multiple_of(240 * t, 240), 240), :],
                push_ref[c],
                (((1,), (1,)), ((), ())),
                preferred_element_type=f32,
            )
            field_ref[c, pl.ds(2 + 6 * t, 6)] += part.reshape(6, EXT, NZ)

        return some

    def sweep(c):
        field = field_ref.at[c]

        def some(t):
            for k in range(6):
                x = 3 + 6 * t + k
                v1_ref[x] = laplace(field, x)
            for k in range(6):
                x = 6 * t + k
                value = laplace(v1_ref, x + 2)
                v2_ref[pl.ds(pl.multiple_of(x * EXT, 8), EXT), :] = value
                next_ref[x, c] = value[4:36]

        return some

    def interpolate(c):
        def some(t):
            columns = pl.ds(pl.multiple_of(t * 1024, 1024), 1024)
            mixed = jnp.dot(across_ref[c], plane_ref[:, columns], preferred_element_type=f32)
            total = jnp.sum(mixed * depth_ref[:, columns], axis=0, keepdims=True)
            for k in range(8):
                sum_ref[pl.ds(64 * c + 8 * t + k, 1), :] = total[:, 128 * k : 128 * k + 128]

        return some

    halos = []

    def send_halo(c):
        copies = []
        for k, side in enumerate(SIDES):
            first, last, low, high = side_range(side)
            strips[k][c] = field_ref[c, first:last, low:high, :].reshape(side_rows(side), NZ).astype(bf16)
            copies.append(send(strips[k].at[c], got[k].at[c], around, 8 * c + k, sides[k]))
        halos.append(copies)

    def receive_halo(c):
        for copy in halos[c]:
            copy.wait_recv()
        for side, strip in zip(SIDES, got):
            first, last, low, high = opposite_range(side)
            part = strip[c].astype(f32).reshape(last - first, high - low, NZ)
            field_ref[c, first:last, low:high, :] += part
        for x in (1, 2):
            v1_ref[x] = laplace(field_ref.at[c], x)

    def turn_over(c):
        for part in range(PADDED // 128):
            piece = v2_ref[128 * part : 128 * part + 128, :]
            across_ref[c, :, 128 * part : 128 * part + 128] = piece.T.astype(bf16)

    pass_over([spread(0)])
    send_halo(0)
    pass_over([spread(1)])
    send_halo(1)
    receive_halo(0)
    pass_over([spread(2), sweep(0)])
    send_halo(2)
    turn_over(0)
    receive_halo(1)
    pass_over([interpolate(0), sweep(1)])
    turn_over(1)
    receive_halo(2)
    pass_over([interpolate(1), sweep(2)])
    turn_over(2)
    own_next = pltpu.make_async_copy(next_ref.at[2:34], next_hbm, bulk.at[2])
    own_next.start()

    def depart(h):
        out_ref[h] = sum_ref[128 * h : 128 * h + 128, :].T.reshape(GY, GX, 128)
        return first_stage("gy", GY, out_ref.at[h], middle_ref.at[h], behind[2 * h], here.at[2 + h])

    def forward(h):
        for b in range(GY):
            about_ref[h, pl.ds(b, GX, stride=GY), :] = middle_ref[h, b]
        turned = about_ref.at[h].reshape(GX, GY, 128)
        return first_stage("gx", GX, turned, back_ref.at[h], behind[2 * h + 1], bulk.at[h])

    def half(first):
        def some(t, _):
            interpolate(2)(t)
            return 0

        lax.fori_loop(first, first + 3, some, 0)

    back = [depart(0)]
    half(0)
    received(back[0])
    back.append(forward(0))
    half(3)
    back.append(depart(1))
    received(back[2])
    back.append(forward(1))
    received(back[1])
    received(back[3])
    own_next.wait()
    for stage in [stage1, stage2] + back:
        sent(stage)
    for copies in halos:
        for copy in copies:
            copy.wait_send()


def step(inputs, velocity):
    dma = pltpu.SemaphoreType.DMA
    strips = [pltpu.VMEM((3, side_rows(side), NZ), bf16) for side in SIDES]
    return pl.pallas_call(
        step_kernel,
        out_shape=[
            jax.ShapeDtypeStruct((CELLS, 3, CELLS, NZ), f32),
            jax.ShapeDtypeStruct((2, GX, GY, 128), f32),
        ],
        in_specs=[ANY] * 6,
        out_specs=[ANY, VMEM],
        scratch_shapes=[
            pltpu.VMEM((3, SLOTS), f32),
            pltpu.VMEM((3, SLOTS), f32),
            pltpu.VMEM((3, SLOTS), i32),
            pltpu.VMEM((CAP, 128), i32),
            pltpu.VMEM((1, DEVICES), i32),
            dma((5,)),
            pltpu.VMEM((DEVICES, DEVICES), i32),
            pltpu.VMEM((CAP, 128), f32),
            pltpu.VMEM((6 * CAP, 128), f32),
            pltpu.VMEM((GX * 48, 128), f32),
            pltpu.VMEM((GX, 48, 128), f32),
            pltpu.VMEM((GY * 24, 128), f32),
            pltpu.VMEM((GY, 24, 128), f32),
            pltpu.VMEM((384, 128), f32),
            pltpu.VMEM((12 * CAP, 128), f32),
            pltpu.VMEM((3 * CAP, 128), i32),
            pltpu.VMEM((PADDED, SLOTS), bf16),
            pltpu.VMEM((3, NZ, SLOTS), bf16),
            pltpu.VMEM((NZ, SLOTS), f32),
            pltpu.VMEM((3, EXT, EXT, NZ), f32),
            pltpu.VMEM((EXT, EXT, NZ), f32),
            pltpu.VMEM((PADDED, NZ), f32),
            pltpu.VMEM((3, NZ, PADDED), bf16),
            pltpu.VMEM((256, 128), f32),
            pltpu.VMEM((2, GY, GX, 128), f32),
            pltpu.VMEM((2, GY, GX, 128), f32),
            pltpu.VMEM((2, DEVICES, 128), f32),
            pltpu.VMEM((CELLS, 3, CELLS, NZ), f32),
            pltpu.VMEM((CELLS + 4, 3, CELLS, NZ), f32),
            *strips,
            *strips,
            dma((GX,)), dma((GX,)), dma((GY,)), dma((GY,)),
            dma((GY,)), dma((GY,)), dma((GX,)), dma((GX,)),
            dma((GY,)), dma((GY,)), dma((GX,)), dma((GX,)),
            dma((24,)), dma((24,)), dma((4,)), dma((4,)),
        ],
        compiler_params=params(61, collective_id=0, has_side_effects=True),
        cost_estimate=pl.CostEstimate(flops=4 * PADDED * SLOTS * 3 * NZ, bytes_accessed=10**7, transcendentals=0),
    )(*inputs, velocity)


def unpack_kernel(back_hbm, counts_hbm, out_ref, back_ref, counts_ref, sems, live_ref, flat_ref):
    fetch([(back_hbm, back_ref), (counts_hbm, counts_ref)], sems)
    live_ref[...] = counts_column(counts_ref)
    lane = lax.broadcasted_iota(i32, (16, 128), 1)
    for c in range(3):
        base = 64 * (c % 2)
        rows = [jnp.zeros((16, 128), f32)] * 3
        for j in range(8):
            row0, lane0 = divmod(CAP * j, 128)
            part = back_ref[pl.ds(DEVICES * (c // 2) + j, 16, stride=8), :]
            part = jnp.where(lane - base < live_ref[pl.ds(j, 16, stride=8), :], part, 0.0)
            shift = (lane0 - base) % 128
            part = pltpu.roll(part, shift, 1) if shift else part
            rows[row0] = jnp.where((lane >= lane0) & (lane < lane0 + CAP), part, rows[row0])
            if lane0 + CAP > 128:
                rows[row0 + 1] = jnp.where(lane < lane0 + CAP - 128, part, rows[row0 + 1])
        for r in range(3):
            flat_ref[pl.ds(c * CAP + r, 16, stride=3), :] = rows[r]
        for r in range(CAP):
            out_ref[c : c + 1, 128 * r : 128 * r + 128] = flat_ref[c * CAP + r : c * CAP + r + 1, :]


def body(velocity, fiber_loads, fractions, corners, neighbours, counts):
    counts = counts.reshape(1, DEVICES)
    dma = pltpu.SemaphoreType.DMA
    inputs = (fiber_loads, fractions, corners, neighbours.reshape(CAP, 128), counts)
    following, back = step(inputs, velocity.transpose(0, 2, 1, 3))
    fiber_velocity = pl.pallas_call(
        unpack_kernel,
        out_shape=jax.ShapeDtypeStruct((3, SLOTS), f32),
        in_specs=[ANY] * 2,
        out_specs=VMEM,
        scratch_shapes=[
            pltpu.VMEM((2 * DEVICES, 128), f32),
            pltpu.VMEM((1, DEVICES), i32),
            dma((2,)),
            pltpu.VMEM((DEVICES, DEVICES), i32),
            pltpu.VMEM((3 * CAP, 128), f32),
        ],
        compiler_params=params(),
    )(back.reshape(2 * DEVICES, 128), counts)
    velocity_next = following.transpose(0, 2, 1, 3)
    return (velocity_next, fiber_velocity)


def solution(mesh):
    return jax.shard_map(
        body,
        mesh=mesh,
        in_specs=(
            P("gx", "gy", None, None),
            P(None, ("gx", "gy")),
            P(None, ("gx", "gy")),
            P(None, ("gx", "gy")),
            P(("gx", "gy")),
            P(("gx", "gy")),
        ),
        out_specs=(P("gx", "gy", None, None), P(None, ("gx", "gy"))),
        check_vma=False,
    )
```

time: 102 us -> 88.2 us (0.86)
  local copies, waits for them, and re-layouts: 12.7 us -> 4.87 us
  Pallas kernels: 88.2 us -> 82.4 us
    pallas_call x2 -> x1, Pallas kernels: 87.1 us -> 81.4 us  [step(): pl.pallas_call(step_kernel, out_shape=[jax.ShapeDtypeStruct((CELLS, 3, CE...]
    reshape x1 -> x0, local copies, waits for them, and re-layouts: 4 us -> none  [body(): velocity_next = following.reshape(3, CELLS, CELLS, NZ).transpose(1, 2, 0, 3)]
    transpose x1 -> x0, local copies, waits for them, and re-layouts: 3.97 us -> none  [body(): mine = velocity.transpose(2, 0, 1, 3).reshape(3 * CELLS, CELLS, NZ)]
    unnamed x16 -> x5, local copies, waits for them, and re-layouts: 4.77 us -> 4.87 us
where the time goes in v2:
time: 88.2 us; the launch traced here: 88 us
  Pallas kernels  82.4 us (93%)
  local copies, waits for them, and re-layouts  4.87 us (6%)
    pallas_call x1, Pallas kernels, step(): pl.pallas_call(step_kernel, out_shape=[jax.ShapeDtypeStruct((CELLS, 3, CE...  81.4 us
    unnamed x5, local copies, waits for them, and re-layouts  4.87 us

profile of v2, /device:TPU:1, one launch (start us, length us, event | category | flops | bytes accessed | tf_op | source)
XLA Modules:
  0.0 88.0 jit_solution(16622351860136050276)
XLA Ops:
  0.6 0.0 copy-start.1
  0.6 81.4 %shard_map.77 = (f32[32,3,32,256]{3,2,1,0:T(8,128)}, f32[2,8,16,128]{3,2,1,0:T(8,128)}) custom-call(f32[3,6144]{1,0:T(4,128)} %refs_0_.1, f32[3,6144]{1,0:T(4,128)} %refs_1_.1, s32[3,6144]{1,0:T(4,128)} %refs_2_.1, s32[48,128]{1,0:T(8,128)} %bitcast.10, s32[1,128]{1,0:T(1,128)} %bitcast.6, f32[32,3,32,256]{3,2,1,0:T(8,128)} %bitcast.9), custom_call_target="tpu_custom_call" | custom-call | flops 28991029248 | bytes 10000000 | tf_op jit(solution)/shard_map/pallas_call | solution.py:399
  82.0 0.0 copy-done.1
  82.0 0.0 copy-start
  82.0 0.9 %copy-done = f32[2,8,16,128]{3,2,1,0:T(8,128)S(1)} copy-done((f32[2,8,16,128]{3,2,1,0:T(8,128)S(1)}, f32[2,8,16,128]{3,2,1,0:T(8,128)}, u32[]{:S(2)}) %copy-start) | copy-done | bytes 131096
  82.9 1.1 %shard_map.78 = f32[3,6144]{1,0:T(4,128)} custom-call(f32[256,128]{1,0:T(8,128)S(1)} %bitcast.5, s32[1,128]{1,0:T(1,128)S(1)} %bitcast.7), custom_call_target="tpu_custom_call" | custom-call | tf_op jit(solution)/shard_map/pallas_call | solution.py:476
  84.0 4.0 %copy.9 = f32[32,32,3,256]{3,1,2,0:T(8,128)} copy(f32[32,32,3,256]{3,1,2,0:T(8,128)} %bitcast.8) | data formatting | bytes 6291456
Async XLA Ops:
  0.6 81.4 %copy-start.1 = (s32[128]{0:T(128)S(1)}, s32[128]{0:T(128)}, u32[]{:S(2)}) copy-start(s32[128]{0:T(128)} %param.11) | copy-start | bytes 1540
  82.0 0.9 %copy-start = (f32[2,8,16,128]{3,2,1,0:T(8,128)S(1)}, f32[2,8,16,128]{3,2,1,0:T(8,128)}, u32[]{:S(2)}) copy-start(f32[2,8,16,128]{3,2,1,0:T(8,128)} %get-tuple-element.5) | copy-start | bytes 393220

commit v3 on v2

--- a/solution.py
+++ b/solution.py
@@ -21,6 +21,7 @@
 MESH = pl.DeviceIdType.MESH
 VMEM = pl.BlockSpec(memory_space=pltpu.VMEM)
 ANY = pl.BlockSpec(memory_space=pl.ANY)
+HBM = pl.BlockSpec(memory_space=pltpu.MemorySpace.HBM)
 f32, bf16, i32 = jnp.float32, jnp.bfloat16, jnp.int32
 
 
@@ -228,13 +229,13 @@
     return first, last, low, high
 
 
-def pass_over(tasks):
+def pass_over(steps, tasks):
     def some(t, _):
         for task in tasks:
             task(t)
         return 0
 
-    lax.fori_loop(0, 6, some, 0)
+    lax.fori_loop(0, steps, some, 0, unroll=True)
 
 
 def step_kernel(*refs):
@@ -282,24 +283,24 @@
     def spread(c):
         def some(t):
             part = lax.dot_general(
-                plane_ref[pl.ds(pl.multiple_of(240 * t, 240), 240), :],
+                plane_ref[pl.ds(pl.multiple_of(720 * t, 720), 720), :],
                 push_ref[c],
                 (((1,), (1,)), ((), ())),
                 preferred_element_type=f32,
             )
-            field_ref[c, pl.ds(2 + 6 * t, 6)] += part.reshape(6, EXT, NZ)
+            field_ref[c, pl.ds(2 + 18 * t, 18)] += part.reshape(18, EXT, NZ)
 
         return some
 
-    def sweep(c):
+    def sweep(c, count):
         field = field_ref.at[c]
 
         def some(t):
-            for k in range(6):
-                x = 3 + 6 * t + k
+            for k in range(count):
+                x = 3 + count * t + k
                 v1_ref[x] = laplace(field, x)
-            for k in range(6):
-                x = 6 * t + k
+            for k in range(count):
+                x = count * t + k
                 value = laplace(v1_ref, x + 2)
                 v2_ref[pl.ds(pl.multiple_of(x * EXT, 8), EXT), :] = value
                 next_ref[x, c] = value[4:36]
@@ -341,19 +342,19 @@
             piece = v2_ref[128 * part : 128 * part + 128, :]
             across_ref[c, :, 128 * part : 128 * part + 128] = piece.T.astype(bf16)
 
-    pass_over([spread(0)])
+    pass_over(2, [spread(0)])
     send_halo(0)
-    pass_over([spread(1)])
+    pass_over(2, [spread(1)])
     send_halo(1)
     receive_halo(0)
-    pass_over([spread(2), sweep(0)])
+    pass_over(2, [spread(2), sweep(0, 18)])
     send_halo(2)
     turn_over(0)
     receive_halo(1)
-    pass_over([interpolate(0), sweep(1)])
+    pass_over(6, [interpolate(0), sweep(1, 6)])
     turn_over(1)
     receive_halo(2)
-    pass_over([interpolate(1), sweep(2)])
+    pass_over(6, [interpolate(1), sweep(2, 6)])
     turn_over(2)
     own_next = pltpu.make_async_copy(next_ref.at[2:34], next_hbm, bulk.at[2])
     own_next.start()
@@ -373,7 +374,7 @@
             interpolate(2)(t)
             return 0
 
-        lax.fori_loop(first, first + 3, some, 0)
+        lax.fori_loop(first, first + 3, some, 0, unroll=True)
 
     back = [depart(0)]
     half(0)
@@ -446,8 +447,26 @@
     )(*inputs, velocity)
 
 
-def unpack_kernel(back_hbm, counts_hbm, out_ref, back_ref, counts_ref, sems, live_ref, flat_ref):
-    fetch([(back_hbm, back_ref), (counts_hbm, counts_ref)], sems)
+PIECES = 8
+
+
+def unpack_kernel(back_hbm, counts_hbm, next_hbm, result_hbm, out_ref, *scratch):
+    back_ref, counts_ref, sems, live_ref, flat_ref, next_ref, in_sems, out_sems = scratch
+    size = CELLS // PIECES
+    pieces = [pl.ds(size * k, size) for k in range(PIECES)]
+    arrive = [pltpu.make_async_copy(next_hbm.at[p], next_ref.at[p], in_sems.at[k]) for k, p in enumerate(pieces)]
+    leave = [pltpu.make_async_copy(next_ref.at[p], result_hbm.at[p], out_sems.at[k]) for k, p in enumerate(pieces)]
+    small = [
+        pltpu.make_async_copy(src, dst, sems.at[k])
+        for k, (src, dst) in enumerate([(back_hbm, back_ref), (counts_hbm, counts_ref)])
+    ]
+    for copy in small + arrive:
+        copy.start()
+    for copy in small:
+        copy.wait()
+    for k in range(PIECES):
+        arrive[k].wait()
+        leave[k].start()
     live_ref[...] = counts_column(counts_ref)
     lane = lax.broadcasted_iota(i32, (16, 128), 1)
     for c in range(3):
@@ -466,6 +485,8 @@
             flat_ref[pl.ds(c * CAP + r, 16, stride=3), :] = rows[r]
         for r in range(CAP):
             out_ref[c : c + 1, 128 * r : 128 * r + 128] = flat_ref[c * CAP + r : c * CAP + r + 1, :]
+    for copy in leave:
+        copy.wait()
 
 
 def body(velocity, fiber_loads, fractions, corners, neighbours, counts):
@@ -473,22 +494,27 @@
     dma = pltpu.SemaphoreType.DMA
     inputs = (fiber_loads, fractions, corners, neighbours.reshape(CAP, 128), counts)
     following, back = step(inputs, velocity.transpose(0, 2, 1, 3))
-    fiber_velocity = pl.pallas_call(
+    velocity_next, fiber_velocity = pl.pallas_call(
         unpack_kernel,
-        out_shape=jax.ShapeDtypeStruct((3, SLOTS), f32),
-        in_specs=[ANY] * 2,
-        out_specs=VMEM,
+        out_shape=[
+            jax.ShapeDtypeStruct((CELLS, 3, CELLS, NZ), f32),
+            jax.ShapeDtypeStruct((3, SLOTS), f32),
+        ],
+        in_specs=[HBM] * 3,
+        out_specs=[HBM, VMEM],
         scratch_shapes=[
             pltpu.VMEM((2 * DEVICES, 128), f32),
             pltpu.VMEM((1, DEVICES), i32),
             dma((2,)),
             pltpu.VMEM((DEVICES, DEVICES), i32),
             pltpu.VMEM((3 * CAP, 128), f32),
+            pltpu.VMEM((CELLS, 3, CELLS, NZ), f32),
+            dma((PIECES,)),
+            dma((PIECES,)),
         ],
-        compiler_params=params(),
-    )(back.reshape(2 * DEVICES, 128), counts)
-    velocity_next = following.transpose(0, 2, 1, 3)
-    return (velocity_next, fiber_velocity)
+        compiler_params=params(61),
+    )(back.reshape(2 * DEVICES, 128), counts, following)
+    return (velocity_next.transpose(0, 2, 1, 3), fiber_velocity)
 
 
 def solution(mesh):

time: 88.2 us -> 81.9 us (0.929)
  local copies, waits for them, and re-layouts: 4.87 us -> 0 us
  Pallas kernels: 82.4 us -> 80.9 us
    unnamed x5 -> x0, local copies, waits for them, and re-layouts: 4.87 us -> none
    pallas_call x1, Pallas kernels: 81.4 us -> 76.8 us  [step(): pl.pallas_call(step_kernel, out_shape=[jax.ShapeDtypeStruct((CELLS, 3, CE...]
    pallas_call x1, Pallas kernels: 1.06 us -> 4.06 us  [body(): pl.pallas_call(unpack_kernel, out_shape=[jax.ShapeDtypeStruct((CELLS, 3,...]
where the time goes in v3:
time: 81.9 us; the launch traced here: 81.7 us
  Pallas kernels  80.9 us (99%)
  between operations  0.84 us (1%)
    pallas_call x1, Pallas kernels, step(): pl.pallas_call(step_kernel, out_shape=[jax.ShapeDtypeStruct((CELLS, 3, CE...  76.8 us
    pallas_call x1, Pallas kernels, body(): pl.pallas_call(unpack_kernel, out_shape=[jax.ShapeDtypeStruct((CELLS, 3,...  4.06 us

profile of v3, /device:TPU:1, one launch (start us, length us, event | category | flops | bytes accessed | tf_op | source)
XLA Modules:
  0.0 81.7 jit_solution(11363846588718939102)
XLA Ops:
  0.6 76.8 %shard_map.77 = (f32[32,3,32,256]{3,2,1,0:T(8,128)}, f32[2,8,16,128]{3,2,1,0:T(8,128)}) custom-call(f32[3,6144]{1,0:T(4,128)} %refs_0_.1, f32[3,6144]{1,0:T(4,128)} %refs_1_.1, s32[3,6144]{1,0:T(4,128)} %refs_2_.1, s32[48,128]{1,0:T(8,128)} %bitcast.10, s32[1,128]{1,0:T(1,128)} %bitcast.6, f32[32,3,32,256]{3,2,1,0:T(8,128)} %bitcast.8), custom_call_target="tpu_custom_call" | custom-call | flops 28991029248 | bytes 10000000 | tf_op jit(solution)/shard_map/pallas_call | solution.py:400
  77.4 4.1 %shard_map.78 = (f32[32,3,32,256]{3,2,1,0:T(8,128)}, f32[3,6144]{1,0:T(4,128)}) custom-call(f32[256,128]{1,0:T(8,128)} %bitcast.5, s32[1,128]{1,0:T(1,128)} %bitcast.7, f32[32,3,32,256]{3,2,1,0:T(8,128)} %get-tuple-element.7.next_hbm), custom_call_target="tpu_custom_call" | custom-call | tf_op jit(solution)/shard_map/pallas_call | solution.py:497

commit v4 on v3

--- a/solution.py
+++ b/solution.py
@@ -229,13 +229,13 @@
     return first, last, low, high
 
 
-def pass_over(steps, tasks):
+def pass_over(steps, tasks, unroll=False):
     def some(t, _):
         for task in tasks:
             task(t)
         return 0
 
-    lax.fori_loop(0, steps, some, 0, unroll=True)
+    lax.fori_loop(0, steps, some, 0, unroll=unroll)
 
 
 def step_kernel(*refs):
@@ -247,8 +247,8 @@
     plane_ref, push_ref, depth_ref, field_ref, v1_ref, v2_ref, across_ref = scratch[16:23]
     sum_ref, out_ref, middle_ref, about_ref, velocity_ref, next_ref = scratch[23:29]
     strips, got, sems = scratch[29:37], scratch[37:45], scratch[45:]
-    ahead, behind, around = (sems[0:2], sems[2:4]), (sems[4:6], sems[6:8], sems[8:10], sems[10:12]), sems[12:14]
-    here, bulk = sems[14], sems[15]
+    ahead, behind, around = (sems[0:2], sems[2:4]), (sems[4:6], sems[6:8], sems[8:10]), sems[10:12]
+    here, bulk = sems[12], sems[13]
 
     gx, gy = lax.axis_index("gx"), lax.axis_index("gy")
     sides = [(lax.rem(gx + dx + GX, GX), lax.rem(gy + dy + GY, GY)) for dx, dy in SIDES]
@@ -351,41 +351,38 @@
     send_halo(2)
     turn_over(0)
     receive_halo(1)
-    pass_over(6, [interpolate(0), sweep(1, 6)])
+    pass_over(6, [interpolate(0), sweep(1, 6)], True)
     turn_over(1)
     receive_halo(2)
-    pass_over(6, [interpolate(1), sweep(2, 6)])
+    pass_over(6, [interpolate(1), sweep(2, 6)], True)
     turn_over(2)
     own_next = pltpu.make_async_copy(next_ref.at[2:34], next_hbm, bulk.at[2])
     own_next.start()
 
     def depart(h):
         out_ref[h] = sum_ref[128 * h : 128 * h + 128, :].T.reshape(GY, GX, 128)
-        return first_stage("gy", GY, out_ref.at[h], middle_ref.at[h], behind[2 * h], here.at[2 + h])
-
-    def forward(h):
-        for b in range(GY):
-            about_ref[h, pl.ds(b, GX, stride=GY), :] = middle_ref[h, b]
-        turned = about_ref.at[h].reshape(GX, GY, 128)
-        return first_stage("gx", GX, turned, back_ref.at[h], behind[2 * h + 1], bulk.at[h])
-
-    def half(first):
-        def some(t, _):
-            interpolate(2)(t)
-            return 0
-
-        lax.fori_loop(first, first + 3, some, 0, unroll=True)
+        return first_stage("gy", GY, out_ref.at[h], middle_ref.at[h], behind[h], here.at[2 + h])
+
+    def forward():
+        for h in range(2):
+            for b in range(GY):
+                about_ref[h, pl.ds(b, GX, stride=GY), :] = middle_ref[h, b]
+        turned = about_ref.reshape(2, GX, GY, 128)
+        own = pltpu.make_async_copy(turned.at[:, gx], back_ref.at[:, gx], bulk.at[0])
+        copies = []
+        for k in range(1, GX):
+            peer = lax.rem(gx + k, GX)
+            copies.append(send(turned.at[:, peer], back_ref.at[:, gx], behind[2], k, {"gx": peer}))
+        own.start()
+        return [own], copies
 
     back = [depart(0)]
-    half(0)
+    pass_over(6, [interpolate(2)], True)
+    back.append(depart(1))
     received(back[0])
-    back.append(forward(0))
-    half(3)
-    back.append(depart(1))
+    received(back[1])
+    back.append(forward())
     received(back[2])
-    back.append(forward(1))
-    received(back[1])
-    received(back[3])
     own_next.wait()
     for stage in [stage1, stage2] + back:
         sent(stage)
@@ -438,8 +435,7 @@
             *strips,
             *strips,
             dma((GX,)), dma((GX,)), dma((GY,)), dma((GY,)),
-            dma((GY,)), dma((GY,)), dma((GX,)), dma((GX,)),
-            dma((GY,)), dma((GY,)), dma((GX,)), dma((GX,)),
+            dma((GY,)), dma((GY,)), dma((GY,)), dma((GY,)), dma((GX,)), dma((GX,)),
             dma((24,)), dma((24,)), dma((4,)), dma((4,)),
         ],
         compiler_params=params(61, collective_id=0, has_side_effects=True),
@@ -447,7 +443,7 @@
     )(*inputs, velocity)
 
 
-PIECES = 8
+PIECES = 16
 
 
 def unpack_kernel(back_hbm, counts_hbm, next_hbm, result_hbm, out_ref, *scratch):

time: 81.9 us -> 80 us (0.977)
  Pallas kernels: 80.9 us -> 79 us
    pallas_call x1, Pallas kernels: 76.8 us -> 74.6 us  [step(): pl.pallas_call(step_kernel, out_shape=[jax.ShapeDtypeStruct((CELLS, 3, CE...]
where the time goes in v4:
time: 80 us; the launch traced here: 79.8 us
  Pallas kernels  79 us (99%)
  between operations  0.82 us (1%)
    pallas_call x1, Pallas kernels, step(): pl.pallas_call(step_kernel, out_shape=[jax.ShapeDtypeStruct((CELLS, 3, CE...  74.6 us
    pallas_call x1, Pallas kernels, body(): pl.pallas_call(unpack_kernel, out_shape=[jax.ShapeDtypeStruct((CELLS, 3,...  4.43 us

profile of v4, /device:TPU:1, one launch (start us, length us, event | category | flops | bytes accessed | tf_op | source)
XLA Modules:
  0.0 79.8 jit_solution(12306830174279394721)
XLA Ops:
  0.6 74.6 %shard_map.77 = (f32[32,3,32,256]{3,2,1,0:T(8,128)}, f32[2,8,16,128]{3,2,1,0:T(8,128)}) custom-call(f32[3,6144]{1,0:T(4,128)} %refs_0_.1, f32[3,6144]{1,0:T(4,128)} %refs_1_.1, s32[3,6144]{1,0:T(4,128)} %refs_2_.1, s32[48,128]{1,0:T(8,128)} %bitcast.10, s32[1,128]{1,0:T(1,128)} %bitcast.6, f32[32,3,32,256]{3,2,1,0:T(8,128)} %bitcast.8), custom_call_target="tpu_custom_call" | custom-call | flops 28991029248 | bytes 10000000 | tf_op jit(solution)/shard_map/pallas_call | solution.py:397
  75.2 4.4 %shard_map.78 = (f32[32,3,32,256]{3,2,1,0:T(8,128)}, f32[3,6144]{1,0:T(4,128)}) custom-call(f32[256,128]{1,0:T(8,128)} %bitcast.5, s32[1,128]{1,0:T(1,128)} %bitcast.7, f32[32,3,32,256]{3,2,1,0:T(8,128)} %get-tuple-element.7.next_hbm), custom_call_target="tpu_custom_call" | custom-call | tf_op jit(solution)/shard_map/pallas_call | solution.py:493

commit v5 on v4

--- a/solution.py
+++ b/solution.py
@@ -148,13 +148,14 @@
 
 def table(wts_ref, cell_ref, dim, block, length):
     corner = point_row(cell_ref, dim * CAP, block)
-    delta = lax.broadcasted_iota(i32, (length, 256), 0) - corner
-    if dim == 2:
-        delta = delta & (NZ - 1)
-    result = jnp.zeros((length, 256), f32)
+    delta = lax.broadcasted_iota(i32, (8, 256), 0) - corner
+    weight = jnp.zeros((8, 256), f32)
     for k in range(4):
-        result = jnp.where(delta == k, point_row(wts_ref, (4 * dim + k) * CAP, block), result)
-    return result
+        weight = jnp.where(delta & 3 == k, point_row(wts_ref, (4 * dim + k) * CAP, block), weight)
+    tiles = length // 8
+    delta = delta[None] + 8 * lax.broadcasted_iota(i32, (tiles, 8, 256), 0)
+    inside = (delta & (NZ - 4 if dim == 2 else -4)) == 0
+    return jnp.where(inside, weight[None], 0.0).reshape(length, 256)
 
 
 def weights(values_ref, wts_ref, cell_ref):
@@ -180,8 +181,7 @@
             plane_ref[80 * i : 80 * i + 80, columns] = both.astype(bf16)
         depth = table(wts_ref, cell_ref, 2, block, NZ)
         depth_ref[:, columns] = depth
-        for c in range(3):
-            push_ref[c, :, columns] = (depth * point_row(values_ref, 64 * c, block)).astype(bf16)
+        push_ref[0, :, columns] = (depth * point_row(values_ref, 0, block)).astype(bf16)
         return 0
 
     lax.fori_loop(0, BLOCKS, fill, 0)
@@ -292,6 +292,16 @@
 
         return some
 
+    def push(c):
+        def some(t):
+            for k in range(BLOCKS // 2):
+                block = BLOCKS // 2 * t + k
+                columns = pl.ds(pl.multiple_of(block * 256, 256), 256)
+                force = point_row(values_ref, 64 * c, block)
+                push_ref[c, :, columns] = (depth_ref[:, columns] * force).astype(bf16)
+
+        return some
+
     def sweep(c, count):
         field = field_ref.at[c]
 
@@ -342,9 +352,9 @@
             piece = v2_ref[128 * part : 128 * part + 128, :]
             across_ref[c, :, 128 * part : 128 * part + 128] = piece.T.astype(bf16)
 
-    pass_over(2, [spread(0)])
+    pass_over(2, [spread(0), push(1)])
     send_halo(0)
-    pass_over(2, [spread(1)])
+    pass_over(2, [spread(1), push(2)])
     send_halo(1)
     receive_halo(0)
     pass_over(2, [spread(2), sweep(0, 18)])
@@ -443,11 +453,11 @@
     )(*inputs, velocity)
 
 
-PIECES = 16
-
-
-def unpack_kernel(back_hbm, counts_hbm, next_hbm, result_hbm, out_ref, *scratch):
-    back_ref, counts_ref, sems, live_ref, flat_ref, next_ref, in_sems, out_sems = scratch
+PIECES = 8
+
+
+def unpack_kernel(back_hbm, counts_hbm, next_hbm, result_hbm, out_hbm, *scratch):
+    back_ref, counts_ref, sems, live_ref, flat_ref, next_ref, in_sems, out_sems, out_ref = scratch
     size = CELLS // PIECES
     pieces = [pl.ds(size * k, size) for k in range(PIECES)]
     arrive = [pltpu.make_async_copy(next_hbm.at[p], next_ref.at[p], in_sems.at[k]) for k, p in enumerate(pieces)]
@@ -460,9 +470,6 @@
         copy.start()
     for copy in small:
         copy.wait()
-    for k in range(PIECES):
-        arrive[k].wait()
-        leave[k].start()
     live_ref[...] = counts_column(counts_ref)
     lane = lax.broadcasted_iota(i32, (16, 128), 1)
     for c in range(3):
@@ -481,7 +488,12 @@
             flat_ref[pl.ds(c * CAP + r, 16, stride=3), :] = rows[r]
         for r in range(CAP):
             out_ref[c : c + 1, 128 * r : 128 * r + 128] = flat_ref[c * CAP + r : c * CAP + r + 1, :]
-    for copy in leave:
+        for k in range(3 * c, min(3 * c + 3, PIECES)):
+            arrive[k].wait()
+            leave[k].start()
+    own = pltpu.make_async_copy(out_ref, out_hbm, sems.at[0])
+    own.start()
+    for copy in leave + [own]:
         copy.wait()
 
 
@@ -497,7 +509,7 @@
             jax.ShapeDtypeStruct((3, SLOTS), f32),
         ],
         in_specs=[HBM] * 3,
-        out_specs=[HBM, VMEM],
+        out_specs=[HBM, HBM],
         scratch_shapes=[
             pltpu.VMEM((2 * DEVICES, 128), f32),
             pltpu.VMEM((1, DEVICES), i32),
@@ -507,6 +519,7 @@
             pltpu.VMEM((CELLS, 3, CELLS, NZ), f32),
             dma((PIECES,)),
             dma((PIECES,)),
+            pltpu.VMEM((3, SLOTS), f32),
         ],
         compiler_params=params(61),
     )(back.reshape(2 * DEVICES, 128), counts, following)

time: 80 us -> 77.5 us (0.969)
  Pallas kernels: 79 us -> 76.5 us
    pallas_call x1, Pallas kernels: 74.6 us -> 72.9 us  [step(): pl.pallas_call(step_kernel, out_shape=[jax.ShapeDtypeStruct((CELLS, 3, CE...]
where the time goes in v5:
time: 77.5 us; the launch traced here: 77.3 us
  Pallas kernels  76.5 us (99%)
  between operations  0.82 us (1%)
    pallas_call x1, Pallas kernels, step(): pl.pallas_call(step_kernel, out_shape=[jax.ShapeDtypeStruct((CELLS, 3, CE...  72.9 us
    pallas_call x1, Pallas kernels, body(): pl.pallas_call(unpack_kernel, out_shape=[jax.ShapeDtypeStruct((CELLS, 3,...  3.66 us

profile of v5, /device:TPU:1, one launch (start us, length us, event | category | flops | bytes accessed | tf_op | source)
XLA Modules:
  0.0 77.3 jit_solution(16828143306790919118)
XLA Ops:
  0.6 72.9 %shard_map.77 = (f32[32,3,32,256]{3,2,1,0:T(8,128)}, f32[2,8,16,128]{3,2,1,0:T(8,128)}) custom-call(f32[3,6144]{1,0:T(4,128)} %refs_0_.1, f32[3,6144]{1,0:T(4,128)} %refs_1_.1, s32[3,6144]{1,0:T(4,128)} %refs_2_.1, s32[48,128]{1,0:T(8,128)} %bitcast.10, s32[1,128]{1,0:T(1,128)} %bitcast.6, f32[32,3,32,256]{3,2,1,0:T(8,128)} %bitcast.8), custom_call_target="tpu_custom_call" | custom-call | flops 28991029248 | bytes 10000000 | tf_op jit(solution)/shard_map/pallas_call | solution.py:407
  73.5 3.7 %shard_map.78 = (f32[32,3,32,256]{3,2,1,0:T(8,128)}, f32[3,6144]{1,0:T(4,128)}) custom-call(f32[256,128]{1,0:T(8,128)} %bitcast.5, s32[1,128]{1,0:T(1,128)} %bitcast.7, f32[32,3,32,256]{3,2,1,0:T(8,128)} %get-tuple-element.7.next_hbm), custom_call_target="tpu_custom_call" | custom-call | tf_op jit(solution)/shard_map/pallas_call | solution.py:505

commit v6 on v5

--- a/solution.py
+++ b/solution.py
@@ -15,7 +15,7 @@
 CELLS = 32
 NZ = 256
 EXT = 40
-ROWS = 36 * EXT
+ROWS = 36 * 36
 PADDED = 1536
 BLOCKS = CAP // 2
 MESH = pl.DeviceIdType.MESH
@@ -146,9 +146,9 @@
     return jnp.concatenate([ref[pl.ds(base + 2 * block, 1), :], ref[pl.ds(base + 2 * block + 1, 1), :]], axis=1)
 
 
-def table(wts_ref, cell_ref, dim, block, length):
+def table(wts_ref, cell_ref, dim, block, length, first=0):
     corner = point_row(cell_ref, dim * CAP, block)
-    delta = lax.broadcasted_iota(i32, (8, 256), 0) - corner
+    delta = lax.broadcasted_iota(i32, (8, 256), 0) + first - corner
     weight = jnp.zeros((8, 256), f32)
     for k in range(4):
         weight = jnp.where(delta & 3 == k, point_row(wts_ref, (4 * dim + k) * CAP, block), weight)
@@ -174,11 +174,14 @@
     def fill(block, _):
         columns = pl.ds(pl.multiple_of(block * 256, 256), 256)
         along_x = table(wts_ref, cell_ref, 0, block, EXT)
-        along_y = table(wts_ref, cell_ref, 1, block, EXT)
-        for i in range(18):
-            x = 2 + 2 * i
-            both = jnp.concatenate([along_y * along_x[x : x + 1], along_y * along_x[x + 1 : x + 2]], axis=0)
-            plane_ref[80 * i : 80 * i + 80, columns] = both.astype(bf16)
+        even_y = table(wts_ref, cell_ref, 1, block, EXT, 2)
+        odd_y = table(wts_ref, cell_ref, 1, block, EXT, -2)
+        for i in range(9):
+            parts = []
+            for x in (2 + 4 * i, 4 + 4 * i):
+                even, odd = along_x[x : x + 1], along_x[x + 1 : x + 2]
+                parts += [even_y[:32] * even, even_y[32:] * even + odd_y[:8] * odd, odd_y[8:] * odd]
+            plane_ref[144 * i : 144 * i + 144, columns] = jnp.concatenate(parts, axis=0).astype(bf16)
         depth = table(wts_ref, cell_ref, 2, block, NZ)
         depth_ref[:, columns] = depth
         push_ref[0, :, columns] = (depth * point_row(values_ref, 0, block)).astype(bf16)
@@ -272,7 +275,7 @@
             turned_ref[pl.ds(8 * pair + a, GY, stride=24), :] = mid_ref[a, 16 * pair : 16 * pair + 16, :]
     stage2 = first_stage("gy", GY, turned_ref.reshape(GY, 24, 128), recv_ref, ahead[1], here.at[1])
     plane_ref[ROWS:, :] = jnp.zeros((PADDED - ROWS, SLOTS), bf16)
-    v2_ref[ROWS:, :] = jnp.zeros((PADDED - ROWS, NZ), f32)
+    v2_ref[18:] = jnp.zeros((4, 72, NZ), f32)
     sum_ref[...] = jnp.zeros((256, 128), f32)
     received(stage2)
     for pair in range(3):
@@ -283,19 +286,20 @@
     def spread(c):
         def some(t):
             part = lax.dot_general(
-                plane_ref[pl.ds(pl.multiple_of(720 * t, 720), 720), :],
+                plane_ref[pl.ds(pl.multiple_of(432 * t, 432), 432), :],
                 push_ref[c],
                 (((1,), (1,)), ((), ())),
                 preferred_element_type=f32,
             )
-            field_ref[c, pl.ds(2 + 18 * t, 18)] += part.reshape(18, EXT, NZ)
+            for k in range(12):
+                field_ref[c, 2 + 12 * t + k, 2:38, :] += part[36 * k : 36 * k + 36]
 
         return some
 
     def push(c):
         def some(t):
-            for k in range(BLOCKS // 2):
-                block = BLOCKS // 2 * t + k
+            for k in range(BLOCKS // 3):
+                block = BLOCKS // 3 * t + k
                 columns = pl.ds(pl.multiple_of(block * 256, 256), 256)
                 force = point_row(values_ref, 64 * c, block)
                 push_ref[c, :, columns] = (depth_ref[:, columns] * force).astype(bf16)
@@ -312,7 +316,7 @@
             for k in range(count):
                 x = count * t + k
                 value = laplace(v1_ref, x + 2)
-                v2_ref[pl.ds(pl.multiple_of(x * EXT, 8), EXT), :] = value
+                v2_ref[count // 2 * t + k // 2, 36 * (k % 2) : 36 * (k % 2) + 36] = value[2:38]
                 next_ref[x, c] = value[4:36]
 
         return some
@@ -349,15 +353,15 @@
 
     def turn_over(c):
         for part in range(PADDED // 128):
-            piece = v2_ref[128 * part : 128 * part + 128, :]
+            piece = v2_ref.reshape(22 * 72, NZ)[128 * part : 128 * part + 128, :]
             across_ref[c, :, 128 * part : 128 * part + 128] = piece.T.astype(bf16)
 
-    pass_over(2, [spread(0), push(1)])
+    pass_over(3, [spread(0), push(1)])
     send_halo(0)
-    pass_over(2, [spread(1), push(2)])
+    pass_over(3, [spread(1), push(2)])
     send_halo(1)
     receive_halo(0)
-    pass_over(2, [spread(2), sweep(0, 18)])
+    pass_over(3, [spread(2), sweep(0, 12)], True)
     send_halo(2)
     turn_over(0)
     receive_halo(1)
@@ -434,7 +438,7 @@
             pltpu.VMEM((NZ, SLOTS), f32),
             pltpu.VMEM((3, EXT, EXT, NZ), f32),
             pltpu.VMEM((EXT, EXT, NZ), f32),
-            pltpu.VMEM((PADDED, NZ), f32),
+            pltpu.VMEM((22, 72, NZ), f32),
             pltpu.VMEM((3, NZ, PADDED), bf16),
             pltpu.VMEM((256, 128), f32),
             pltpu.VMEM((2, GY, GX, 128), f32),

time: 77.5 us -> 77.7 us (level)
  no operation moved by 1% of the time
where the time goes in v6:
time: 77.7 us; the launch traced here: 77.5 us
  Pallas kernels  76.7 us (99%)
  between operations  0.82 us (1%)
    pallas_call x1, Pallas kernels, step(): pl.pallas_call(step_kernel, out_shape=[jax.ShapeDtypeStruct((CELLS, 3, CE...  73.1 us
    pallas_call x1, Pallas kernels, body(): pl.pallas_call(unpack_kernel, out_shape=[jax.ShapeDtypeStruct((CELLS, 3,...  3.66 us

profile of v6, /device:TPU:1, one launch (start us, length us, event | category | flops | bytes accessed | tf_op | source)
XLA Modules:
  0.0 77.5 jit_solution(8271390760132118375)
XLA Ops:
  0.6 73.1 %shard_map.77 = (f32[32,3,32,256]{3,2,1,0:T(8,128)}, f32[2,8,16,128]{3,2,1,0:T(8,128)}) custom-call(f32[3,6144]{1,0:T(4,128)} %refs_0_.1, f32[3,6144]{1,0:T(4,128)} %refs_1_.1, s32[3,6144]{1,0:T(4,128)} %refs_2_.1, s32[48,128]{1,0:T(8,128)} %bitcast.10, s32[1,128]{1,0:T(1,128)} %bitcast.6, f32[32,3,32,256]{3,2,1,0:T(8,128)} %bitcast.8), custom_call_target="tpu_custom_call" | custom-call | flops 28991029248 | bytes 10000000 | tf_op jit(solution)/shard_map/pallas_call | solution.py:411
  73.7 3.7 %shard_map.78 = (f32[32,3,32,256]{3,2,1,0:T(8,128)}, f32[3,6144]{1,0:T(4,128)}) custom-call(f32[256,128]{1,0:T(8,128)} %bitcast.5, s32[1,128]{1,0:T(1,128)} %bitcast.7, f32[32,3,32,256]{3,2,1,0:T(8,128)} %get-tuple-element.7.next_hbm), custom_call_target="tpu_custom_call" | custom-call | tf_op jit(solution)/shard_map/pallas_call | solution.py:509

commit v7 on v6

--- a/solution.py
+++ b/solution.py
@@ -139,7 +139,7 @@
 
 def side_rows(side):
     dx, dy = side
-    return 6 * EXT if dy == 0 else 36 * 8 if dx == 0 else 6 * 8
+    return 6 * EXT if dy == 0 else 224 if dx == 0 else 6 * 8
 
 
 def point_row(ref, base, block):
@@ -337,7 +337,12 @@
         copies = []
         for k, side in enumerate(SIDES):
             first, last, low, high = side_range(side)
-            strips[k][c] = field_ref[c, first:last, low:high, :].reshape(side_rows(side), NZ).astype(bf16)
+            if side[0] == 0:
+                low = 2 if side[1] < 0 else 32
+                parts = [field_ref[c, x, low : low + 6, :] for x in range(2, 38)] + [jnp.zeros((8, NZ), f32)]
+                strips[k][c] = jnp.concatenate(parts, axis=0).astype(bf16)
+            else:
+                strips[k][c] = field_ref[c, first:last, low:high, :].reshape(side_rows(side), NZ).astype(bf16)
             copies.append(send(strips[k].at[c], got[k].at[c], around, 8 * c + k, sides[k]))
         halos.append(copies)
 
@@ -346,8 +351,13 @@
             copy.wait_recv()
         for side, strip in zip(SIDES, got):
             first, last, low, high = opposite_range(side)
-            part = strip[c].astype(f32).reshape(last - first, high - low, NZ)
-            field_ref[c, first:last, low:high, :] += part
+            part = strip[c].astype(f32)
+            if side[0] == 0:
+                low = 34 if side[1] < 0 else 0
+                for x in range(36):
+                    field_ref[c, 2 + x, low : low + 6, :] += part[6 * x : 6 * x + 6]
+            else:
+                field_ref[c, first:last, low:high, :] += part.reshape(last - first, high - low, NZ)
         for x in (1, 2):
             v1_ref[x] = laplace(field_ref.at[c], x)
 

time: 77.7 us -> 77.2 us (level)
  no operation moved by 1% of the time
where the time goes in v7:
time: 77.2 us; the launch traced here: 77.1 us
  Pallas kernels  76.3 us (99%)
  between operations  0.82 us (1%)
    pallas_call x1, Pallas kernels, step(): pl.pallas_call(step_kernel, out_shape=[jax.ShapeDtypeStruct((CELLS, 3, CE...  72.6 us
    pallas_call x1, Pallas kernels, body(): pl.pallas_call(unpack_kernel, out_shape=[jax.ShapeDtypeStruct((CELLS, 3,...  3.66 us

profile of v7, /device:TPU:1, one launch (start us, length us, event | category | flops | bytes accessed | tf_op | source)
XLA Modules:
  0.0 77.1 jit_solution(10066992199025230975)
XLA Ops:
  0.6 72.6 %shard_map.77 = (f32[32,3,32,256]{3,2,1,0:T(8,128)}, f32[2,8,16,128]{3,2,1,0:T(8,128)}) custom-call(f32[3,6144]{1,0:T(4,128)} %refs_0_.1, f32[3,6144]{1,0:T(4,128)} %refs_1_.1, s32[3,6144]{1,0:T(4,128)} %refs_2_.1, s32[48,128]{1,0:T(8,128)} %bitcast.10, s32[1,128]{1,0:T(1,128)} %bitcast.6, f32[32,3,32,256]{3,2,1,0:T(8,128)} %bitcast.8), custom_call_target="tpu_custom_call" | custom-call | flops 28991029248 | bytes 10000000 | tf_op jit(solution)/shard_map/pallas_call | solution.py:421
  73.3 3.7 %shard_map.78 = (f32[32,3,32,256]{3,2,1,0:T(8,128)}, f32[3,6144]{1,0:T(4,128)}) custom-call(f32[256,128]{1,0:T(8,128)} %bitcast.5, s32[1,128]{1,0:T(1,128)} %bitcast.7, f32[32,3,32,256]{3,2,1,0:T(8,128)} %get-tuple-element.7.next_hbm), custom_call_target="tpu_custom_call" | custom-call | tf_op jit(solution)/shard_map/pallas_call | solution.py:519
